TPU v7x, 256 devices: a whole 4x4x8 slice. The times are simulated.
256 devices in a mesh: dp: 32 (over x, z), tp: 8 (over y, core).
Axes of the slice: x: 4, y: 4, z: 8, core: 2. Of those that a mesh axis runs over, the one named last changes fastest.
Arguments:
- queries: bfloat16 [512, 128, 576], P('dp', 'tp'), may hold values from -22.5 to 22.5
- new_latent: bfloat16 [512, 576], P('dp'), may hold values from -4.5 to 4.5
- residual: bfloat16 [512, 7168], P('dp', 'tp'), may hold values from -11 to 11
- pool: bfloat16 [4096, 64, 576], P('dp', 'tp'), may hold values from -4.5 to 4.5
- page_owner: int32 [512, 4], P('dp'), may hold values from 0 to 31, as said below
- page_slot: int32 [512, 4], P('dp'), may hold values from 0 to 127, as said below
- lengths: int32 [512], P('dp'), may hold values from 1 to 256, as said below
- resumed: int32 [512], P('dp'), may hold values from 0 to 1, as said below
- value_up: bfloat16 [128, 512, 128], P('tp'), may hold values from -0.25 to 0.25
- out_proj: bfloat16 [16384, 7168], P('dp', 'tp'), may hold values from -0.19921875 to 0.19921875
- norm_gain: float32 [7168], P('tp'), may hold values from 0.1 to 1.9
- gate_weight: bfloat16 [7168, 18432], P('tp', 'dp'), may hold values from -0.0625 to 0.0625
- up_weight: bfloat16 [7168, 18432], P('tp', 'dp'), may hold values from -0.0625 to 0.0625
- down_weight: bfloat16 [18432, 7168], P('dp', 'tp'), may hold values from -0.046875 to 0.046875
Outputs:
- layer_out: bfloat16 [512, 7168], P('dp', 'tp')
Inputs may be any that keep to these rules, and one draw needn't show every extreme that they name: `page_owner`: request i is served by rank floor(i / 16). A page p of request i is read when resumed[i] = 1 and p * 64 < lengths[i]. Among the pages of one rank's requests at most 4 have any one owner, and at most 2 of the read ones; in every draw and on every rank some owner holds exactly 4 of them, 2 of them read. `page_slot`: no two pages of any requests share one owner's slot. `lengths`: some request has exactly 256 tokens. `resumed`: the requests of one rank read at most 32 pages in all; some rank reads exactly 32.
All inputs are finite; a program needn't handle non-finite values.
Results may differ from a plain program's by a relative error of at most 0.018.
Values may be sent and summed in bfloat16 or wider, within the bound.
A program may use at most 64 MiB of HBM per device.

v0:
```python
import jax
import jax.numpy as jnp
from jax import lax
from jax.sharding import PartitionSpec as P

D = 7168
KL = 512
PAGE = 64


SCORE_SCALE = 192.0 ** (-0.5)
EPSILON = 1e-06


def fetch_pages(pool, page_owner, page_slot):
    rank_count = lax.axis_size("dp")
    req_rows, page_count = page_owner.shape
    ref_count = req_rows * page_count
    capacity = 2 * ref_count // rank_count
    owners = page_owner.reshape(ref_count)
    slots_used = page_slot.reshape(ref_count)
    positions = jnp.arange(ref_count, dtype=jnp.int32)
    earlier = (owners[:, None] == owners[None, :]) & (positions[:, None] > positions[None, :])
    copy_rank = jnp.sum(earlier.astype(jnp.int32), axis=1)
    wanted = jnp.zeros((rank_count, capacity), jnp.int32).at[owners, copy_rank].set(slots_used)
    located = jnp.take(
        pool, lax.all_to_all(wanted, "dp", split_axis=0, concat_axis=0, tiled=True), axis=0
    )
    fetched = lax.all_to_all(located, "dp", split_axis=0, concat_axis=0, tiled=True)
    local_pages = fetched[owners, copy_rank]
    return local_pages.reshape((req_rows, page_count) + local_pages.shape[1:])


def attend_pages(queries, new_latent, local_pages, lengths, resumed):
    req_rows, head_count, columns = queries.shape
    page_count = local_pages.shape[1]
    own_score = (
        jnp.einsum("rhc,rc->rh", queries, new_latent, preferred_element_type=jnp.float32)
        * SCORE_SCALE
    )
    context_end = jnp.where(resumed == 1, lengths, 0)
    own_latent = new_latent[:, :KL].astype(jnp.float32)
    portion = lax.all_gather(local_pages, "tp", axis=2, tiled=True)
    running_top = own_score
    weight_sum = jnp.ones_like(own_score)
    latent_sum = jnp.broadcast_to(own_latent[:, None, :], (req_rows, head_count, KL))
    piece_len = portion.shape[2]
    scores = (
        jnp.einsum("rhc,rptc->rhpt", queries, portion, preferred_element_type=jnp.float32)
        * SCORE_SCALE
    )
    position = (
        jnp.arange(page_count, dtype=jnp.int32)[:, None] * PAGE
        + jnp.arange(piece_len, dtype=jnp.int32)[None, :]
    )
    usable = (position[None, :, :] < context_end[:, None, None])[:, None, :, :]
    piece_peak = jnp.max(jnp.where(usable, scores, running_top[:, :, None, None]), axis=(2, 3))
    new_top = jnp.maximum(running_top, piece_peak)
    weights = jnp.where(usable, jnp.exp(scores - new_top[:, :, None, None]), 0.0)
    rescale = jnp.exp(running_top - new_top)
    weight_sum = weight_sum * rescale + jnp.sum(weights, axis=(2, 3))
    latent_sum = latent_sum * rescale[:, :, None] + jnp.einsum(
        "rhpt,rptc->rhc",
        weights.astype(jnp.bfloat16),
        portion[..., :KL],
        preferred_element_type=jnp.float32,
    )
    running_top, weight_sum, latent_sum = (new_top, weight_sum, latent_sum)
    return (latent_sum / weight_sum[:, :, None]).astype(jnp.bfloat16)


def per_device(
    queries,
    new_latent,
    residual,
    pool,
    page_owner,
    page_slot,
    lengths,
    resumed,
    value_up,
    out_proj,
    norm_gain,
    gate_weight,
    up_weight,
    down_weight,
):
    req_rows = queries.shape[0]
    local_pages = fetch_pages(pool, page_owner, page_slot)
    latent_out = attend_pages(queries, new_latent, local_pages, lengths, resumed)
    heads_out = jnp.einsum("rhc,hcv->rhv", latent_out, value_up, preferred_element_type=jnp.float32)
    heads_out = heads_out.astype(jnp.bfloat16).reshape(req_rows, -1)
    all_heads = lax.all_gather(heads_out, "tp", axis=1, tiled=True)
    head_block = lax.all_to_all(all_heads, "dp", split_axis=1, concat_axis=0, tiled=True)
    attended = lax.psum_scatter(
        jnp.dot(head_block, out_proj, preferred_element_type=jnp.float32).astype(jnp.bfloat16),
        "dp",
        scatter_dimension=0,
        tiled=True,
    ).astype(jnp.float32)
    stream = lax.optimization_barrier(
        (residual.astype(jnp.float32) + attended).astype(jnp.bfloat16)
    )
    widened = stream.astype(jnp.float32)
    squares = lax.psum(jnp.sum(widened * widened, axis=1), "tp")
    normalize_widened = stream.astype(jnp.float32)
    normed = (normalize_widened * lax.rsqrt(squares[:, None] / D + EPSILON) * norm_gain).astype(
        jnp.bfloat16
    )
    inputs = lax.all_gather(normed, "dp", axis=0, tiled=True)
    products = jnp.concatenate(
        (
            jnp.dot(inputs, gate_weight, preferred_element_type=jnp.float32),
            jnp.dot(inputs, up_weight, preferred_element_type=jnp.float32),
        ),
        axis=1,
    )
    half_width = products.shape[1] // 2
    summed = lax.psum(products.astype(jnp.bfloat16), "tp").astype(jnp.float32)
    hidden = (jax.nn.silu(summed[:, :half_width]) * summed[:, half_width:]).astype(jnp.bfloat16)
    lowered = jnp.dot(hidden, down_weight, preferred_element_type=jnp.float32)
    lowered_sum = lax.psum_scatter(
        lowered.astype(jnp.bfloat16), "dp", scatter_dimension=0, tiled=True
    ).astype(jnp.float32)
    return (widened + lowered_sum).astype(jnp.bfloat16)


def solution(mesh):
    return jax.shard_map(
        per_device,
        mesh=mesh,
        in_specs=(
            P("dp", "tp", None),
            P("dp", None),
            P("dp", "tp"),
            P("dp", "tp", None),
            P("dp", None),
            P("dp", None),
            P("dp"),
            P("dp"),
            P("tp", None, None),
            P("dp", "tp"),
            P("tp"),
            P("tp", "dp"),
            P("tp", "dp"),
            P("dp", "tp"),
        ),
        out_specs=P("dp", "tp"),
        check_vma=False,
    )
```

profile of v0, /device:TPU:1, one launch (start us, length us, event | category | flops | bytes accessed | tf_op | source)
XLA Modules:
  0.0 682.9 jit_solution(10368993576212536860)
XLA Ops:
  6.5 0.9 copy.44
  7.4 0.1 eq.19
  7.5 0.1 reshape.130
  7.6 0.2 convert_reduce_fusion
  7.8 0.8 copy.46
  8.6 0.1 reshape.150
  8.7 3.5 scatter_fusion
  12.2 0.7 copy.47
  12.9 11.9 %all-to-all-start = ((s32[32,1,4]{2,1,0:T(1,128)}), s32[32,1,4]{2,1,0:T(1,128)S(1)}, u32[]{:S(2)}, u32[]{:S(2)}) async-start(s32[32,1,4]{2,1,0:T(1,128)} %copy.47), calls=%async_computation | async-start | bytes 32768 | tf_op jit(solution)/shard_map/all_to_all | solution.py:27
  24.8 2.2 copy.52
  27.0 6.3 all-to-all-done
  33.3 0.1 copy.48
  33.4 0.1 copy.49
  33.5 0.1 copy.51
  33.6 0.1 reshape.136
  33.7 1.8 gather_fusion
  35.5 1.6 broadcast_select_fusion
  37.1 34.1 %all_to_all.39 = bf16[32,4,8,576]{3,2,1,0:T(8,128)(2,1)S(1)} all-to-all(bf16[32,4,8,576]{3,2,1,0:T(8,128)(2,1)S(1)} %broadcast_select_fusion), channel_id=1, replica_groups=mesh['dp'=32,'tp'=8] {'dp'}, dimensions={0} | all-to-all | bytes 2359296 | tf_op jit(solution)/shard_map/all_to_all | solution.py:29
  71.2 1.6 gather_fusion.1
  72.9 0.0 reduce-scatter.3.cloned.1.call-start
  73.0 0.1 iota_add_fusion
  73.0 0.1 broadcast_compare_fusion
  73.1 1.2 fusion.27
  74.3 38.3 %all-gather.2.cloned.1.call-done = bf16[16,4,64,576]{3,2,1,0:T(8,128)(2,1)} async-done(((bf16[16,4,8,576]{3,2,1,0:T(8,128)(2,1)}), bf16[16,4,64,576]{3,2,1,0:T(8,128)(2,1)}) %all-gather.2.cloned.1.call-update) | async-done | bytes 4718608 | tf_op jit(solution)/shard_map/all_gather | solution.py:43
  112.6 5.3 select_reduce_fusion
  117.9 0.3 bitcast_reduce_fusion
  118.2 0.9 fusion.13
  119.1 0.5 fusion.9
  119.6 13.3 %all_gather.10 = bf16[16,16384]{1,0:T(8,128)(2,1)S(1)} all-gather(bf16[16,2048]{1,0:T(8,128)(2,1)S(1)} %bitcast.75), channel_id=1, replica_groups=mesh['dp'=32,'tp'=8] {'tp'}, dimensions={1}, use_global_device_ids=true | all-gather | bytes 589824 | tf_op jit(solution)/shard_map/all_gather | solution.py:93
  132.9 0.1 copy.68
  133.0 24.1 %all_to_all.40 = bf16[16,32,512]{2,0,1:T(8,128)(2,1)S(1)} all-to-all(bf16[16,32,512]{2,0,1:T(8,128)(2,1)S(1)} %bitcast.73), channel_id=1, replica_groups=mesh['dp'=32,'tp'=8] {'dp'}, dimensions={1} | all-to-all | bytes 1048576 | tf_op jit(solution)/shard_map/all_to_all | solution.py:94
  157.1 1.6 convolution_convert_fusion.1
  158.8 187.9 %reduce-scatter.3.cloned.1.call-done = bf16[16,896]{1,0:T(8,128)(2,1)} async-done(((bf16[512,896]{1,0:T(8,128)(2,1)}), bf16[16,896]{1,0:T(8,128)(2,1)}) %reduce-scatter.3.cloned.1.call-update) | async-done | bytes 28688 | tf_op jit(solution)/shard_map/reduce_scatter | solution.py:95
  346.8 0.8 add_convert_fusion
  347.5 0.1 fusion.23
  347.6 17.8 %psum.14 = f32[16]{0:T(128)S(1)} all-reduce(f32[16]{0:T(128)S(1)} %fusion.23), channel_id=1, replica_groups=mesh['dp'=32,'tp'=8] {'tp'}, use_global_device_ids=true, to_apply=%region_6.7 | all-reduce | flops 16 | bytes 128 | tf_op jit(solution)/shard_map/psum | solution.py:105
  365.5 0.1 fusion.25
  365.6 37.1 %all_gather.11 = bf16[512,896]{1,0:T(8,128)(2,1)S(1)} all-gather(bf16[16,896]{1,0:T(8,128)(2,1)S(1)} %fusion.25), channel_id=1, replica_groups=mesh['dp'=32,'tp'=8] {'dp'}, dimensions={0}, use_global_device_ids=true | all-gather | bytes 946176 | tf_op jit(solution)/shard_map/all_gather | solution.py:110
  402.6 0.8 convolution_convert_fusion.2
  403.5 0.4 copy-done.7
  403.9 0.8 convolution_convert_fusion.3
  404.7 1.1 pad_maximum_fusion
  405.8 0.0 reduce-scatter.5.cloned.1.call-start
  405.9 74.0 %all-reduce.2.cloned.1.call-done = bf16[512,1152]{0,1:T(8,128)(2,1)} async-done(((bf16[512,1152]{0,1:T(8,128)(2,1)}), bf16[512,1152]{0,1:T(8,128)(2,1)}) %all-reduce.2.cloned.1.call-update) | async-done | bytes 1179664 | tf_op jit(solution)/shard_map/psum | solution.py:119
  479.9 1.6 convert_element_type.65
  481.5 2.0 convolution_convert_fusion
  483.4 191.6 %reduce-scatter.5.cloned.1.call-done = bf16[16,896]{1,0:T(8,128)(2,1)} async-done(((bf16[512,896]{1,0:T(8,128)(2,1)}), bf16[16,896]{1,0:T(8,128)(2,1)}) %reduce-scatter.5.cloned.1.call-update) | async-done | bytes 28688 | tf_op jit(solution)/shard_map/reduce_scatter | solution.py:122
  675.0 1.4 fusion.26
  (42 shorter events, 0.3 us)
Async XLA Ops:
  6.5 112.5 %copy-start = (bf16[16,512,128]{2,1,0:T(8,128)(2,1)S(1)}, bf16[16,512,128]{2,1,0:T(8,128)(2,1)}, u32[]{:S(2)}) copy-start(bf16[16,512,128]{2,1,0:T(8,128)(2,1)} %param.22) | copy-start | bytes 6291460
  12.9 20.4 %all-to-all-start = ((s32[32,1,4]{2,1,0:T(1,128)}), s32[32,1,4]{2,1,0:T(1,128)S(1)}, u32[]{:S(2)}, u32[]{:S(2)}) async-start(s32[32,1,4]{2,1,0:T(1,128)} %copy.47), calls=%async_computation | async-start | bytes 32768 | tf_op jit(solution)/shard_map/all_to_all | solution.py:27
  24.8 87.8 %all-gather.2.cloned.1.call-start = ((), (), s32[]{:S(2)}) async-start(), calls=%async_computation.5 | async-start | bytes 5898240 | tf_op jit(solution)/shard_map/all_gather | solution.py:43
  71.2 1.7 copy-start.10
  71.2 1.7 copy-start.11
  71.2 1.9 copy-start.4
  72.8 39.8 %copy-start.2 = (bf16[16,16,576]{2,1,0:T(8,128)(2,1)S(1)}, bf16[16,16,576]{2,1,0:T(8,128)(2,1)}, u32[]{:S(2)}) copy-start(bf16[16,16,576]{2,1,0:T(8,128)(2,1)} %param.14) | copy-start | bytes 884740
  72.9 273.9 %reduce-scatter.3.cloned.1.call-start = ((), (), s32[]{:S(2)}) async-start(), calls=%async_computation.6 | async-start | bytes 946176 | tf_op jit(solution)/shard_map/reduce_scatter | solution.py:95
  112.6 5.6 copy-start.1
  119.6 37.5 %copy-start.9 = (bf16[512,896]{1,0:T(8,128)(2,1)S(1)}, bf16[512,896]{1,0:T(8,128)(2,1)}, u32[]{:S(2)}) copy-start(bf16[512,896]{1,0:T(8,128)(2,1)} %param.23) | copy-start | bytes 2752516
  157.1 189.7 %copy-start.3 = (bf16[16,896]{1,0:T(8,128)(2,1)S(1)}, bf16[16,896]{1,0:T(8,128)(2,1)}, u32[]{:S(2)}) copy-start(bf16[16,896]{1,0:T(8,128)(2,1)} %param.16) | copy-start | bytes 86020
  157.1 208.4 %copy-start.5 = (f32[896]{0:T(1024)S(1)}, f32[896]{0:T(1024)}, u32[]{:S(2)}) copy-start(f32[896]{0:T(1024)} %param.24) | copy-start | bytes 10756
  158.8 243.9 %copy-start.6 = (bf16[896,576]{0,1:T(8,128)(2,1)S(1)}, bf16[896,576]{0,1:T(8,128)(2,1)}, u32[]{:S(2)}) copy-start(bf16[896,576]{0,1:T(8,128)(2,1)} %param.26) | copy-start | bytes 3096580
  158.8 321.1 %all-reduce.2.cloned.1.call-start = ((), (), s32[]{:S(2)}) async-start(), calls=%async_computation.7 | async-start | bytes 2359296 | tf_op jit(solution)/shard_map/psum | solution.py:119
  402.6 1.2 copy-start.7
  405.8 75.6 %copy-start.8 = (bf16[576,896]{1,0:T(8,128)(2,1)S(1)}, bf16[576,896]{1,0:T(8,128)(2,1)}, u32[]{:S(2)}) copy-start(bf16[576,896]{1,0:T(8,128)(2,1)} %param.27) | copy-start | bytes 3096580
  405.8 269.2 %reduce-scatter.5.cloned.1.call-start = ((), (), s32[]{:S(2)}) async-start(), calls=%async_computation.8 | async-start | bytes 946176 | tf_op jit(solution)/shard_map/reduce_scatter | solution.py:122
Sparse Core Ops, SparseCore 0:
  73.0 39.5 all-gather.1
  158.9 187.8 reduce-scatter.2
  405.9 73.8 all-reduce.1
  483.8 191.1 reduce-scatter.4
where the time goes:
time: 688 us; the launch traced here: 683 us
  waiting for transfers between devices  498 us (72%)
  blocking collectives  127 us (18%)
  between operations  13.4 us (2%)
  matrix products  13 us (2%)
  local copies, waits for them, and re-layouts  12.6 us (2%)
  starting transfers between devices  12 us (2%)
  other arithmetic  7.27 us (1%)
    reduce_scatter x1, waiting for transfers between devices, per_device(): lax.psum_scatter(lowered.astype(jnp.bfloat16), 'dp', scatter_dimension=0,...  192 us
    reduce_scatter x1, waiting for transfers between devices, per_device(): lax.psum_scatter(jnp.dot(head_block, out_proj, preferred_element_type=jnp...  188 us
    psum x1, waiting for transfers between devices, per_device(): summed = lax.psum(products.astype(jnp.bfloat16), 'tp').astype(jnp.float32)  74 us
    all_gather x1, waiting for transfers between devices, attend_pages(): portion = lax.all_gather(local_pages, 'tp', axis=2, tiled=True)  38.3 us
    all_gather x1, blocking collectives, per_device(): inputs = lax.all_gather(normed, 'dp', axis=0, tiled=True)  37.1 us
    all_to_all x1, blocking collectives, fetch_pages(): lax.all_to_all(located, 'dp', split_axis=0, concat_axis=0, tiled=True)  34.1 us
    all_to_all x1, blocking collectives, per_device(): lax.all_to_all(all_heads, 'dp', split_axis=1, concat_axis=0, tiled=True)  24.1 us
    psum x1, blocking collectives, per_device(): squares = lax.psum(jnp.sum(widened * widened, axis=1), 'tp')  17.8 us
  transfers between devices with their start and end apart: 5, of which 5 were waited for; matrix products, arithmetic and copies ran while one was open for 1% of the time, Pallas kernels for 0%

commit v1 on v0

v1 whole, which is shorter than its diff:
```python
import functools

import jax
import jax.numpy as jnp
from jax import lax
from jax.experimental import pallas as pl
from jax.experimental.pallas import tpu as pltpu
from jax.sharding import PartitionSpec as P

MESH = pl.DeviceIdType.MESH
F32, BF16, I32 = jnp.float32, jnp.bfloat16, jnp.int32

NX, NY, NZ, NC = 4, 4, 8, 2
REQ_D = 16
HEADS = 16
COLS = 576
KL = 512
VH = 128
TOK = 8
PAGE = 64
PAGES = 4
USED = 32
WIDTH = 896
FFD = 576
D = 7168
SCORE_SCALE = 192.0 ** (-0.5)
EPSILON = 1e-06

FAR_Z = (4, 3, 5, 2, 6, 1, 7)
FAR_X = (2, 1, 3)
FAR_Y = (2, 1, 3)
FAR_DP = sorted(
    ((dx, dz) for dx in range(NX) for dz in range(NZ) if dx or dz),
    key=lambda o: -(min(o[0], NX - o[0]) + min(o[1], NZ - o[1])),
)


def send(src, dst, send_sem, recv_sem, device):
    copy = pltpu.make_async_remote_copy(
        src_ref=src,
        dst_ref=dst,
        send_sem=send_sem,
        recv_sem=recv_sem,
        device_id=device,
        device_id_type=MESH,
    )
    copy.start()


def wait_bytes(ref, sem):
    pltpu.make_async_copy(ref, ref, sem).wait()


def column(row, n):
    rows = lax.broadcasted_iota(I32, (n, n), 0)
    lanes = lax.broadcasted_iota(I32, (n, n), 1)
    return jnp.sum(jnp.where(rows == lanes, row, 0), axis=1, keepdims=True)


def dot(a, b):
    return jnp.dot(a, b, preferred_element_type=F32)


def dot_t(a, b):
    return lax.dot_general(a, b, (((1,), (1,)), ((), ())), preferred_element_type=F32)


def kernel(
    owner_ref, slot_ref, len_ref, res_ref, nl_ref, resid_ref, gain_ref,
    q_hbm, pool_hbm, vup_hbm, wo_hbm, wg_hbm, wu_hbm, wd_hbm,
    out_ref,
    q_v, pool_v, vup_v, wo_v, wg_v, wu_v, wd_v, load_sem,
    want_v, asked_v, asked_s, sel_v, sel_s, limit_v, smem_sem, req_ss, req_rs,
    pg_send, pg_recv, pg_ss, pg_rs,
    keys, key_ss, key_rs, sib_ss, sib_rs,
    qt_v, scores_v,
    hd_send, hd_in, hd_ss, hd_rs,
    hb, hb_ss, hb_rs, hs_ss, hs_rs,
    px_send, px_recv, px_ss, px_rs, pz_own, pz_send, pz_recv, pz_ss, pz_rs,
    stream_v, gat, gz_ss, gz_rs, gx_ss, gx_rs,
    act_v, ssq_send, ssq_recv, ssq_ss, ssq_rs,
    gs_own, gs_send, gs_recv, gs_ss, gs_rs,
    gy_own, gy_send, gy_recv, gy_ss, gy_rs,
    hid, hy_ss, hy_rs, hc_ss, hc_rs,
    dx_send, dx_recv, dx_ss, dx_rs, dz_own, dz_send, dz_recv, dz_ss, dz_rs,
):
    dp, tp = lax.axis_index("dp"), lax.axis_index("tp")
    x, z = dp // NZ, dp % NZ
    y, c = tp // NC, tp % NC

    def at(dx=0, dz=0, dy=0, flip=False):
        core = 1 - c if flip else c
        return (((x + dx) % NX) * NZ + (z + dz) % NZ, ((y + dy) % NY) * NC + core)

    loads = [
        pltpu.make_async_copy(src, dst, load_sem.at[i])
        for i, (src, dst) in enumerate(
            [(pool_hbm, pool_v), (q_hbm, q_v), (vup_hbm, vup_v), (wo_hbm, wo_v),
             (wg_hbm, wg_v), (wu_hbm, wu_v), (wd_hbm, wd_v)]
        )
    ]
    for load in loads:
        load.start()

    barrier = pltpu.get_barrier_semaphore()
    for ox, oz in FAR_DP:
        pl.semaphore_signal(barrier, 1, device_id=at(ox, oz), device_id_type=MESH)
    for oy in FAR_Y:
        pl.semaphore_signal(barrier, 1, device_id=at(dy=oy), device_id_type=MESH)
    pl.semaphore_signal(barrier, 1, device_id=at(flip=True), device_id_type=MESH)
    in_tp = dp // 4
    to_self = jnp.where((tp == in_tp) & (z % 2 == c), 1, 0)

    def greet(k, carry):
        source = 2 * k + c

        @pl.when(jnp.logical_not((source == dp) & (in_tp == tp)))
        def _():
            pl.semaphore_signal(barrier, 1, device_id=(source, in_tp), device_id_type=MESH)

        return carry

    lax.fori_loop(0, 16, greet, 0)

    lengths = column(len_ref[...], REQ_D)
    resumed = column(res_ref[...], REQ_D)
    before = (
        lax.broadcasted_iota(I32, (REQ_D, REQ_D, 1), 1) < lax.broadcasted_iota(I32, (REQ_D, REQ_D, 1), 0)
    ).astype(I32)

    def earlier(v):
        return jnp.sum(before * v[None], axis=1)

    lane = lax.broadcasted_iota(I32, (REQ_D, 128), 1)
    lane_owner = lane % 32
    lane_copy = lane // 32
    page_lane = lax.broadcasted_iota(I32, (REQ_D, USED * TOK), 1) // TOK
    owner_base = jnp.zeros((1, 128), I32)
    read_base = jnp.zeros((1, 128), I32)
    wanted = jnp.zeros((1, 128), I32)
    limit = jnp.zeros((REQ_D, USED * TOK), I32)
    chosen = jnp.zeros((1, USED * TOK), I32)
    for p in range(PAGES):
        owner = owner_ref[:, p : p + 1]
        read = jnp.where((resumed == 1) & (lengths > p * PAGE), 1, 0)
        match = jnp.where(lane_owner == owner, read, 0)
        copy = owner_base + earlier(match)
        owner_base = owner_base + jnp.sum(match, axis=0, keepdims=True)
        wanted = wanted + jnp.sum(
            jnp.where((match > 0) & (copy == lane_copy), slot_ref[:, p : p + 1], 0), axis=0, keepdims=True
        )
        own_copy = jnp.sum(jnp.where(lane < 32, match * copy, 0), axis=1, keepdims=True)
        read_lanes = jnp.broadcast_to(read, (REQ_D, 128))
        place = (read_base + earlier(read_lanes))[:, 0:1]
        read_base = read_base + jnp.sum(read_lanes, axis=0, keepdims=True)
        here = jnp.where(page_lane == place, read, 0)
        limit = limit + here * (lengths - p * PAGE)
        off_x = (x - owner // NZ + NX) % NX
        off_z = (z - owner % NZ + NZ) % NZ
        source = (off_x * NZ + off_z) * 2 + own_copy
        chosen = chosen + jnp.sum(here * source, axis=0, keepdims=True)
    limit_v[...] = limit.astype(F32)
    want_v[0] = wanted
    asked_v[0] = wanted
    sel_v[0] = chosen
    sel_copy = pltpu.make_async_copy(sel_v, sel_s, smem_sem.at[0])
    sel_copy.start()

    pl.semaphore_wait(barrier, 31 + 4 + 16 - to_self)

    for ox, oz in FAR_DP:
        send(want_v.at[0], asked_v.at[ox * NZ + oz], req_ss, req_rs, at(ox, oz))

    loads[1].wait()
    rows = lax.broadcasted_iota(I32, (256, 256), 0)
    lanes = lax.broadcasted_iota(I32, (256, 256), 1)
    swap = jnp.where(lanes == (rows % 16) * 16 + rows // 16, 1.0, 0.0).astype(BF16)
    qt = dot(swap, q_v[...]).astype(BF16)
    qt_v[...] = qt
    own_all = dot_t(qt, nl_ref[...]) * SCORE_SCALE
    own_diag = lax.broadcasted_iota(I32, (256, 16), 1) == lax.broadcasted_iota(I32, (256, 16), 0) % 16
    own_score = jnp.sum(jnp.where(own_diag, own_all, 0.0), axis=1, keepdims=True)
    loads[0].wait()
    sel_copy.wait()

    wait_bytes(asked_v.at[pl.ds(1, 31)], req_rs)
    asked_copy = pltpu.make_async_copy(asked_v, asked_s, smem_sem.at[1])
    asked_copy.start()
    asked_copy.wait()

    def gather(n_in, buffer, n_out):
        pair = [pool_v[jnp.clip(asked_s[n_in, 0, 32 * k + dp], 0, 127)] for k in range(2)]
        buffer[n_out] = jnp.concatenate(pair, axis=0)

    for ox, oz in FAR_DP:
        n_out = ox * NZ + oz
        gather(((NX - ox) % NX) * NZ + (NZ - oz) % NZ, pg_send, n_out)
        send(pg_send.at[n_out], pg_recv.at[n_out], pg_ss, pg_rs, at(ox, oz))
    gather(0, pg_recv, 0)
    wait_bytes(pg_recv.at[pl.ds(1, 31)], pg_rs)

    def pick(u, carry):
        pair = []
        for k in range(2):
            source = jnp.clip(sel_s[0, 0, (2 * u + k) * TOK], 0, 63)
            both = pg_recv[lax.shift_right_logical(source, 1)]
            pair.append(jnp.where(jnp.bitwise_and(source, 1) == 1, both[TOK:], both[:TOK]))
        keys[0, pl.ds(pl.multiple_of(u * 16, 16), 16), :] = jnp.concatenate(pair, axis=0)
        return carry

    lax.fori_loop(0, USED // 2, pick, 0)
    for oy in FAR_Y:
        send(keys.at[0], keys.at[oy], key_ss, key_rs.at[oy], at(dy=oy))
    send(keys.at[0], keys.at[4], sib_ss, sib_rs.at[0], at(flip=True))

    qt = qt_v[...]
    limit = limit_v[...].reshape(1, REQ_D, USED * TOK)
    token = (lax.broadcasted_iota(I32, (1, 1, USED * TOK), 2) % TOK).astype(F32)

    def score_block(n, source_tp):
        block = (dot_t(qt, keys[n]) * SCORE_SCALE).reshape(HEADS, REQ_D, USED * TOK)
        usable = limit > token + (source_tp * TOK).astype(F32)
        block = jnp.where(usable, block, -jnp.inf)
        scores_v[n] = block.reshape(256, USED * TOK)

    def source_of(n):
        core = c if n < 4 else 1 - c
        return ((y + NY - n % 4) % NY) * NC + core

    score_block(0, source_of(0))
    for oy in (1, 3, 2):
        wait_bytes(keys.at[oy], key_rs.at[oy])
        send(keys.at[oy], keys.at[4 + oy], sib_ss, sib_rs.at[oy], at(flip=True))
        score_block(oy, source_of(oy))
    for oy in (0, 1, 3, 2):
        wait_bytes(keys.at[4 + oy], sib_rs.at[oy])
        score_block(4 + oy, source_of(4 + oy))

    peak = scores_v[0]
    for n in range(1, 8):
        peak = jnp.maximum(peak, scores_v[n])
    top = jnp.maximum(own_score, jnp.max(peak, axis=1, keepdims=True))
    own_weight = jnp.exp(own_score - top)
    weight_lanes = jnp.zeros((256, USED * TOK), F32)
    latent = jnp.zeros((256, KL), F32)
    for n in range(8):
        weights = jnp.exp(scores_v[n] - top)
        weight_lanes = weight_lanes + weights
        latent = latent + dot(weights.astype(BF16), keys[n, :, :KL])
    weight_sum = own_weight + jnp.sum(weight_lanes, axis=1, keepdims=True)
    own_latent = nl_ref[:, :KL].astype(F32).reshape(1, REQ_D, KL)
    latent = latent.reshape(HEADS, REQ_D, KL) + own_weight.reshape(HEADS, REQ_D, 1) * own_latent
    latent = (latent / weight_sum.reshape(HEADS, REQ_D, 1)).astype(BF16)

    loads[2].wait()
    for h in range(HEADS):
        hd_send[h] = dot(latent[h], vup_v[h]).astype(BF16)
        target = (4 * tp + h // 4, (h % 4) * NC + z % 2)
        is_me = (target[0] == dp) & (target[1] == tp)

        @pl.when(is_me)
        def _():
            pltpu.make_async_copy(hd_send.at[h], hd_in.at[dp // 2], hd_rs).start()

        @pl.when(jnp.logical_not(is_me))
        def _():
            send(hd_send.at[h], hd_in.at[dp // 2], hd_ss, hd_rs, target)

    wait_bytes(hd_in, hd_rs)
    own_cols = pl.ds(pl.multiple_of(y * VH, VH), VH)
    hb[:, pl.ds(c, 1), :, own_cols] = hd_in[...].reshape(NX, 1, 64, VH)
    own_block = hb.at[:, c, :, own_cols]
    for oy in FAR_Y:
        send(own_block, own_block, hb_ss, hb_rs.at[oy], at(dy=oy))
    send(own_block, own_block, hs_ss, hs_rs.at[0], at(flip=True))
    for oy in (1, 3, 2):
        cols = pl.ds(pl.multiple_of(((y + NY - oy) % NY) * VH, VH), VH)
        block = hb.at[:, c, :, cols]
        wait_bytes(block, hb_rs.at[oy])
        send(block, block, hs_ss, hs_rs.at[oy], at(flip=True))
    for oy in range(4):
        wait_bytes(own_block, hs_rs.at[oy])

    def reduce_scatter(rows_of, weight, place, x_send, x_recv, x_ss, x_rs, z_own, z_send, z_recv, z_ss, z_rs):
        for ox in FAR_X:
            x_send[ox - 1] = dot(rows_of((x + ox) % NX), weight).astype(BF16)
            send(x_send.at[ox - 1], x_recv.at[ox - 1], x_ss, x_rs, at(dx=ox))
        total = dot(rows_of(x), weight)
        wait_bytes(x_recv, x_rs)
        for n in range(3):
            total = total + x_recv[n].astype(F32)
        total = total.reshape(NZ, REQ_D, WIDTH)
        z_own[...] = total
        z_send[...] = total.astype(BF16)
        for oz in FAR_Z:
            send(z_send.at[place((z + oz) % NZ)], z_recv.at[oz - 1], z_ss, z_rs, at(dz=oz))
        mine = z_own[place(z)]
        wait_bytes(z_recv, z_rs)
        for n in range(7):
            mine = mine + z_recv[n].astype(F32)
        return mine

    loads[3].wait()
    attended = reduce_scatter(
        lambda xx: hb[xx].reshape(128, 512), wo_v[...], lambda zz: (zz % 2) * 4 + zz // 2,
        px_send, px_recv, px_ss, px_rs, pz_own, pz_send, pz_recv, pz_ss, pz_rs,
    )
    stream = (resid_ref[...].astype(F32) + attended).astype(BF16)
    stream_v[...] = stream

    gat[x, z] = stream
    for oz in FAR_Z:
        send(gat.at[x, z], gat.at[x, z], gz_ss, gz_rs, at(dz=oz))
    wait_bytes(gat.at[x, pl.ds(0, 7)], gz_rs)
    for ox in FAR_X:
        send(gat.at[x], gat.at[x], gx_ss, gx_rs.at[ox - 1], at(dx=ox))

    def widen(xx):
        block = gat[xx].reshape(128, WIDTH).astype(F32)
        act_v[xx] = (block * gain_ref[...]).astype(BF16)
        square = block * block
        high = square.astype(BF16)
        low = (square - high.astype(F32)).astype(BF16)
        ones = jnp.ones((8, WIDTH), BF16)
        ssq_send[xx] = dot_t(ones, high) + dot_t(ones, low)

    widen(x)
    for ox in (1, 3, 2):
        xx = (x + NX - ox) % NX
        wait_bytes(gat.at[xx], gx_rs.at[ox - 1])
        widen(xx)
    for n, (oy, flip) in enumerate([(2, True), (2, False), (1, True), (3, True), (1, False), (3, False), (0, True)]):
        send(ssq_send, ssq_recv.at[n], ssq_ss, ssq_rs, at(dy=oy, flip=flip))

    loads[4].wait()
    loads[5].wait()

    def products(half):
        act = act_v[pl.ds(half * 2, 2)].reshape(256, WIDTH)
        return dot(act, wg_v[...]), dot(act, wu_v[...])

    gate, up = products(1 - c)
    gs_send[0] = gate.astype(BF16)
    gs_send[1] = up.astype(BF16)
    send(gs_send, gs_recv, gs_ss, gs_rs, at(flip=True))
    gate, up = products(c)
    gs_own[0] = gate.reshape(NY, 64, FFD)
    gs_own[1] = up.reshape(NY, 64, FFD)
    wait_bytes(gs_recv, gs_rs)
    for oy in FAR_Y:
        yy = (y + oy) % NY
        for k in range(2):
            pair = gs_own[k, yy] + gs_recv[k, pl.ds(pl.multiple_of(yy * 64, 64), 64), :].astype(F32)
            gy_send[oy - 1, k] = pair.astype(BF16)
        send(gy_send.at[oy - 1], gy_recv.at[oy - 1], gy_ss, gy_rs, at(dy=oy))
    gate, up = (
        gs_own[k, y] + gs_recv[k, pl.ds(pl.multiple_of(y * 64, 64), 64), :].astype(F32) for k in range(2)
    )
    wait_bytes(ssq_recv, ssq_rs)
    squares = ssq_send[...]
    for n in range(7):
        squares = squares + ssq_recv[n]
    row_id = lax.broadcasted_iota(I32, (64, 128), 0) + c * 256 + y * 64
    lane_id = lax.broadcasted_iota(I32, (64, 128), 1)
    mean = jnp.zeros((64, 1), F32)
    for n in range(NX):
        mean = mean + jnp.sum(
            jnp.where(row_id == lane_id + 128 * n, squares[n, 0:1, :], 0.0), axis=1, keepdims=True
        )
    scale = lax.rsqrt(mean / D + EPSILON)
    wait_bytes(gy_recv, gy_rs)
    for n in range(3):
        gate = gate + gy_recv[n, 0].astype(F32)
        up = up + gy_recv[n, 1].astype(F32)
    gate = gate * scale
    hidden = (gate / (1.0 + jnp.exp(-gate)) * (up * scale)).astype(BF16)

    hid[c, y] = hidden
    for oy in FAR_Y:
        send(hid.at[c, y], hid.at[c, y], hy_ss, hy_rs.at[oy - 1], at(dy=oy))
    send(hid.at[c, y], hid.at[c, y], hc_ss, hc_rs, at(flip=True))
    for oy in (1, 3, 2):
        yy = (y + NY - oy) % NY
        wait_bytes(hid.at[c, yy], hy_rs.at[oy - 1])
        send(hid.at[c, yy], hid.at[c, yy], hc_ss, hc_rs, at(flip=True))
    wait_bytes(hid.at[1 - c], hc_rs)

    loads[6].wait()
    lowered = reduce_scatter(
        lambda xx: hid[xx // 2, pl.ds((xx % 2) * 2, 2)].reshape(128, FFD), wd_v[...], lambda zz: zz,
        dx_send, dx_recv, dx_ss, dx_rs, dz_own, dz_send, dz_recv, dz_ss, dz_rs,
    )
    out_ref[...] = (stream_v[...].astype(F32) + lowered).astype(BF16)

    wait_bytes(asked_v.at[pl.ds(1, 31)], req_ss)
    wait_bytes(pg_send.at[pl.ds(1, 31)], pg_ss)
    wait_bytes(keys.at[pl.ds(0, 3)], key_ss)
    wait_bytes(keys.at[pl.ds(0, 4)], sib_ss)
    wait_bytes(hd_in.at[pl.ds(0, 15)], hd_ss)

    @pl.when(to_self == 0)
    def _():
        wait_bytes(hd_in.at[0], hd_ss)

    for _ in range(3):
        wait_bytes(own_block, hb_ss)
    for _ in range(4):
        wait_bytes(own_block, hs_ss)
    wait_bytes(px_recv, px_ss)
    wait_bytes(pz_recv, pz_ss)
    wait_bytes(gat.at[x, pl.ds(0, 7)], gz_ss)
    wait_bytes(gat.at[pl.ds(0, 3)], gx_ss)
    wait_bytes(ssq_recv, ssq_ss)
    wait_bytes(gs_send, gs_ss)
    wait_bytes(gy_send, gy_ss)
    wait_bytes(hid.at[0, pl.ds(0, 3)], hy_ss)
    wait_bytes(hid.at[0], hc_ss)
    wait_bytes(dx_recv, dx_ss)
    wait_bytes(dz_recv, dz_ss)


def per_device(
    queries, new_latent, residual, pool, page_owner, page_slot, lengths, resumed,
    value_up, out_proj, norm_gain, gate_weight, up_weight, down_weight,
):
    vmem = pl.BlockSpec(memory_space=pltpu.VMEM)
    anywhere = pl.BlockSpec(memory_space=pl.ANY)
    dma, V = pltpu.SemaphoreType.DMA, pltpu.VMEM
    one = dma
    rs_scratch = [
        V((3, 128, WIDTH), BF16), V((3, 128, WIDTH), BF16), one, one,
        V((NZ, REQ_D, WIDTH), F32), V((NZ, REQ_D, WIDTH), BF16), V((7, REQ_D, WIDTH), BF16), one, one,
    ]
    scratch = [
        V((256, COLS), BF16), V((128, TOK, COLS), BF16), V((HEADS, KL, VH), BF16), V((512, WIDTH), BF16),
        V((WIDTH, FFD), BF16), V((WIDTH, FFD), BF16), V((FFD, WIDTH), BF16), dma((7,)),
        V((1, 1, 128), I32), V((32, 1, 128), I32), pltpu.SMEM((32, 1, 128), I32),
        V((1, 1, 256), I32), pltpu.SMEM((1, 1, 256), I32), V((REQ_D, 256), F32), dma((2,)), one, one,
        V((32, 16, COLS), BF16), V((32, 16, COLS), BF16), one, one,
        V((8, 256, COLS), BF16), one, dma((4,)), one, dma((4,)),
        V((256, COLS), BF16), V((8, 256, 256), F32),
        V((HEADS, 16, VH), BF16), V((16, 16, VH), BF16), one, one,
        V((NX, NC, 64, 512), BF16), one, dma((4,)), one, dma((4,)),
        *rs_scratch,
        V((REQ_D, WIDTH), BF16), V((NX, NZ, REQ_D, WIDTH), BF16), one, one, one, dma((3,)),
        V((NX, 128, WIDTH), BF16), V((NX, 8, 128), F32), V((7, NX, 8, 128), F32), one, one,
        V((2, NY, 64, FFD), F32), V((2, 256, FFD), BF16), V((2, 256, FFD), BF16), one, one,
        V((8, 128), F32), V((3, 2, 64, FFD), BF16), V((3, 2, 64, FFD), BF16), one, one,
        V((NC, NY, 64, FFD), BF16), one, dma((3,)), one, one,
        *rs_scratch,
    ]
    return pl.pallas_call(
        kernel,
        out_shape=jax.ShapeDtypeStruct((REQ_D, WIDTH), BF16),
        in_specs=[vmem] * 7 + [anywhere] * 7,
        out_specs=vmem,
        scratch_shapes=scratch,
        compiler_params=pltpu.CompilerParams(
            collective_id=0, has_side_effects=True, vmem_limit_bytes=56 * 1024 * 1024
        ),
        name="layer",
    )(
        page_owner, page_slot, lengths.reshape(1, REQ_D), resumed.reshape(1, REQ_D), new_latent, residual,
        norm_gain.reshape(1, WIDTH), queries.reshape(256, COLS), pool, value_up, out_proj,
        gate_weight, up_weight, down_weight,
    )


def solution(mesh):
    return jax.shard_map(
        per_device,
        mesh=mesh,
        in_specs=(
            P("dp", "tp", None), P("dp", None), P("dp", "tp"), P("dp", "tp", None), P("dp", None), P("dp", None),
            P("dp"), P("dp"), P("tp", None, None), P("dp", "tp"), P("tp"), P("tp", "dp"), P("tp", "dp"),
            P("dp", "tp"),
        ),
        out_specs=P("dp", "tp"),
        check_vma=False,
    )
```

time: 688 us -> 162 us (0.24)
  waiting for transfers between devices: 498 us -> 0 us
  Pallas kernels: 0 us -> 150 us
  blocking collectives: 127 us -> 0 us
  between operations: 13.4 us -> 0.01 us
  matrix products: 13 us -> 0 us
  starting transfers between devices: 12 us -> 0 us
  other arithmetic: 7.27 us -> 0 us
    reduce_scatter x2 -> x0, waiting for transfers between devices: 380 us -> none  [the longest x1 192 us: per_device(): lax.psum_scatter(lowered.astype(jnp.bfloat16), 'dp', scatter_dimension=0,...]
    pallas_call x0 -> x1, Pallas kernels: none -> 150 us  [per_device(): pl.pallas_call(kernel, out_shape=jax.ShapeDtypeStruct((REQ_D, WIDTH), BF1...]
    psum x1 -> x0, waiting for transfers between devices: 74 us -> none  [per_device(): summed = lax.psum(products.astype(jnp.bfloat16), 'tp').astype(jnp.float32)]
    all_to_all x2 -> x0, blocking collectives: 58.3 us -> none  [the longest x1 34.1 us: fetch_pages(): lax.all_to_all(located, 'dp', split_axis=0, concat_axis=0, tiled=True)]
    all_gather x2 -> x0, blocking collectives: 50.4 us -> none  [the longest x1 37.1 us: per_device(): inputs = lax.all_gather(normed, 'dp', axis=0, tiled=True)]
    all_gather x1 -> x0, waiting for transfers between devices: 38.3 us -> none  [attend_pages(): portion = lax.all_gather(local_pages, 'tp', axis=2, tiled=True)]
    psum x1 -> x0, blocking collectives: 17.8 us -> none  [per_device(): squares = lax.psum(jnp.sum(widened * widened, axis=1), 'tp')]
    dot_general x8 -> x0, matrix products: 13 us -> none  [the longest x1 5.26 us: attend_pages(): jnp.einsum('rhc,rptc->rhpt', queries, portion, preferred_element_type=jnp...]
  transfers between devices with their start and end apart: 5 -> 0, of which waited for: 5 -> 0; matrix products, arithmetic and copies ran while one was open for 1% -> 0% of each run, Pallas kernels for 0% -> 0%
where the time goes in v1:
time: 162 us; the launch traced here: 161 us
  Pallas kernels  150 us (93%)
  local copies, waits for them, and re-layouts  11.2 us (7%)
    pallas_call x1, Pallas kernels, per_device(): pl.pallas_call(kernel, out_shape=jax.ShapeDtypeStruct((REQ_D, WIDTH), BF1...  150 us
    unnamed x10, local copies, waits for them, and re-layouts  9.86 us

profile of v1, /device:TPU:1, one launch (start us, length us, event | category | flops | bytes accessed | tf_op | source)
XLA Modules:
  0.0 161.4 jit_solution(2143673083729389694)
XLA Ops:
  0.0 0.0 copy-start.1
  0.0 1.4 reshape.14.gain_ref
  1.4 1.4 copy.15.owner_ref
  2.7 1.4 copy.16.slot_ref
  4.1 2.4 %copy.18.wg_hbm = bf16[896,576]{1,0:T(8,128)(2,1)} copy(bf16[896,576]{0,1:T(8,128)(2,1)} %param.25) | data formatting | bytes 2064384 | tf_op args[11]
  6.4 0.0 copy-done.1
  6.4 0.0 copy-start
  6.4 1.4 copy.19.wu_hbm
  7.9 0.0 copy-done
  7.9 2.0 %copy.17.pool_hbm = bf16[128,8,576]{2,1,0:T(8,128)(2,1)} copy(bf16[128,8,576]{0,2,1:T(8,128)(2,1)S(1)} %copy-done) | data formatting | bytes 2359296 | tf_op args[3]
  9.9 150.2 %layer.1 = bf16[16,896]{1,0:T(8,128)(2,1)} custom-call(s32[16,4]{1,0:T(8,128)} %copy.15.owner_ref, s32[16,4]{1,0:T(8,128)} %copy.16.slot_ref, s32[1,16]{1,0:T(1,128)} %bitcast.4, s32[1,16]{1,0:T(1,128)} %bitcast.5, bf16[16,576]{1,0:T(8,128)(2,1)} %nl_ref.1, bf16[16,896]{1,0:T(8,128)(2,1)} %resid_ref.1, f32[1,896]{1,0:T(1,128)} %reshape.14.gain_ref, ...), custom_call_target="tpu_custom_call" | custom-call | tf_op jit(solution)/shard_map/layer/pallas_call | solution.py:452
  160.1 1.4 copy.21
Async XLA Ops:
  0.0 6.4 %copy-start.1 = (bf16[896,576]{0,1:T(8,128)(2,1)S(1)}, bf16[896,576]{0,1:T(8,128)(2,1)}, u32[]{:S(2)}) copy-start(bf16[896,576]{0,1:T(8,128)(2,1)} %param.26) | copy-start | bytes 3096580
  6.4 1.4 copy-start

commit v2 on v1

--- a/solution.py
+++ b/solution.py
@@ -69,7 +69,7 @@
     owner_ref, slot_ref, len_ref, res_ref, nl_ref, resid_ref, gain_ref,
     q_hbm, pool_hbm, vup_hbm, wo_hbm, wg_hbm, wu_hbm, wd_hbm,
     out_ref,
-    q_v, pool_v, vup_v, wo_v, wg_v, wu_v, wd_v, load_sem,
+    q_v, pool_t, pool_v, vup_v, wo_v, wgu_v, wd_v, load_sem,
     want_v, asked_v, asked_s, sel_v, sel_s, limit_v, smem_sem, req_ss, req_rs,
     pg_send, pg_recv, pg_ss, pg_rs,
     keys, key_ss, key_rs, sib_ss, sib_rs,
@@ -80,7 +80,7 @@
     stream_v, gat, gz_ss, gz_rs, gx_ss, gx_rs,
     act_v, ssq_send, ssq_recv, ssq_ss, ssq_rs,
     gs_own, gs_send, gs_recv, gs_ss, gs_rs,
-    gy_own, gy_send, gy_recv, gy_ss, gy_rs,
+    gy_send, gy_recv, gy_ss, gy_rs,
     hid, hy_ss, hy_rs, hc_ss, hc_rs,
     dx_send, dx_recv, dx_ss, dx_rs, dz_own, dz_send, dz_recv, dz_ss, dz_rs,
 ):
@@ -95,12 +95,17 @@
     loads = [
         pltpu.make_async_copy(src, dst, load_sem.at[i])
         for i, (src, dst) in enumerate(
-            [(pool_hbm, pool_v), (q_hbm, q_v), (vup_hbm, vup_v), (wo_hbm, wo_v),
-             (wg_hbm, wg_v), (wu_hbm, wu_v), (wd_hbm, wd_v)]
+            [(pool_hbm, pool_t), (q_hbm, q_v), (vup_hbm, vup_v), (wo_hbm, wo_v),
+             (wg_hbm, wgu_v.at[pl.ds(0, FFD)]), (wu_hbm, wgu_v.at[pl.ds(FFD, FFD)]), (wd_hbm, wd_v)]
         )
     ]
     for load in loads:
         load.start()
+    ends = []
+
+    def later(ref, sem):
+        ends.append(lambda: wait_bytes(ref, sem))
+
 
     barrier = pltpu.get_barrier_semaphore()
     for ox, oz in FAR_DP:
@@ -141,13 +146,14 @@
     limit = jnp.zeros((REQ_D, USED * TOK), I32)
     chosen = jnp.zeros((1, USED * TOK), I32)
     for p in range(PAGES):
-        owner = owner_ref[:, p : p + 1]
+        owner = column(owner_ref[p : p + 1, :], REQ_D)
         read = jnp.where((resumed == 1) & (lengths > p * PAGE), 1, 0)
         match = jnp.where(lane_owner == owner, read, 0)
         copy = owner_base + earlier(match)
         owner_base = owner_base + jnp.sum(match, axis=0, keepdims=True)
         wanted = wanted + jnp.sum(
-            jnp.where((match > 0) & (copy == lane_copy), slot_ref[:, p : p + 1], 0), axis=0, keepdims=True
+            jnp.where((match > 0) & (copy == lane_copy), column(slot_ref[p : p + 1, :], REQ_D), 0),
+            axis=0, keepdims=True,
         )
         own_copy = jnp.sum(jnp.where(lane < 32, match * copy, 0), axis=1, keepdims=True)
         read_lanes = jnp.broadcast_to(read, (REQ_D, 128))
@@ -170,6 +176,7 @@
 
     for ox, oz in FAR_DP:
         send(want_v.at[0], asked_v.at[ox * NZ + oz], req_ss, req_rs, at(ox, oz))
+    later(asked_v.at[pl.ds(1, 31)], req_ss)
 
     loads[1].wait()
     rows = lax.broadcasted_iota(I32, (256, 256), 0)
@@ -181,6 +188,13 @@
     own_diag = lax.broadcasted_iota(I32, (256, 16), 1) == lax.broadcasted_iota(I32, (256, 16), 0) % 16
     own_score = jnp.sum(jnp.where(own_diag, own_all, 0.0), axis=1, keepdims=True)
     loads[0].wait()
+    token_row = lax.broadcasted_iota(I32, (1024, 128), 0)
+    slot_lane = lax.broadcasted_iota(I32, (1024, 128), 1)
+    pages = jnp.zeros((1024, COLS), F32)
+    for j in range(TOK):
+        spread = jnp.where(token_row == slot_lane * TOK + j, 1.0, 0.0).astype(BF16)
+        pages = pages + dot_t(spread, pool_t[j])
+    pool_v[...] = pages.astype(BF16).reshape(128, TOK, COLS)
     sel_copy.wait()
 
     wait_bytes(asked_v.at[pl.ds(1, 31)], req_rs)
@@ -196,6 +210,7 @@
         n_out = ox * NZ + oz
         gather(((NX - ox) % NX) * NZ + (NZ - oz) % NZ, pg_send, n_out)
         send(pg_send.at[n_out], pg_recv.at[n_out], pg_ss, pg_rs, at(ox, oz))
+    later(pg_send.at[pl.ds(1, 31)], pg_ss)
     gather(0, pg_recv, 0)
     wait_bytes(pg_recv.at[pl.ds(1, 31)], pg_rs)
 
@@ -212,6 +227,8 @@
     for oy in FAR_Y:
         send(keys.at[0], keys.at[oy], key_ss, key_rs.at[oy], at(dy=oy))
     send(keys.at[0], keys.at[4], sib_ss, sib_rs.at[0], at(flip=True))
+    later(keys.at[pl.ds(0, 3)], key_ss)
+    later(keys.at[pl.ds(0, 4)], sib_ss)
 
     qt = qt_v[...]
     limit = limit_v[...].reshape(1, REQ_D, USED * TOK)
@@ -266,6 +283,15 @@
         def _():
             send(hd_send.at[h], hd_in.at[dp // 2], hd_ss, hd_rs, target)
 
+    def heads_left():
+        wait_bytes(hd_in.at[pl.ds(0, 15)], hd_ss)
+
+        @pl.when(to_self == 0)
+        def _():
+            wait_bytes(hd_in.at[0], hd_ss)
+
+    ends.append(heads_left)
+
     wait_bytes(hd_in, hd_rs)
     own_cols = pl.ds(pl.multiple_of(y * VH, VH), VH)
     hb[:, pl.ds(c, 1), :, own_cols] = hd_in[...].reshape(NX, 1, 64, VH)
@@ -273,6 +299,8 @@
     for oy in FAR_Y:
         send(own_block, own_block, hb_ss, hb_rs.at[oy], at(dy=oy))
     send(own_block, own_block, hs_ss, hs_rs.at[0], at(flip=True))
+    later(hb.at[:, pl.ds(0, 1), :, pl.ds(0, 3 * VH)], hb_ss)
+    later(hb.at[:, 0], hs_ss)
     for oy in (1, 3, 2):
         cols = pl.ds(pl.multiple_of(((y + NY - oy) % NY) * VH, VH), VH)
         block = hb.at[:, c, :, cols]
@@ -285,6 +313,7 @@
         for ox in FAR_X:
             x_send[ox - 1] = dot(rows_of((x + ox) % NX), weight).astype(BF16)
             send(x_send.at[ox - 1], x_recv.at[ox - 1], x_ss, x_rs, at(dx=ox))
+        later(x_send, x_ss)
         total = dot(rows_of(x), weight)
         wait_bytes(x_recv, x_rs)
         for n in range(3):
@@ -294,6 +323,7 @@
         z_send[...] = total.astype(BF16)
         for oz in FAR_Z:
             send(z_send.at[place((z + oz) % NZ)], z_recv.at[oz - 1], z_ss, z_rs, at(dz=oz))
+        later(z_recv, z_ss)
         mine = z_own[place(z)]
         wait_bytes(z_recv, z_rs)
         for n in range(7):
@@ -311,13 +341,15 @@
     gat[x, z] = stream
     for oz in FAR_Z:
         send(gat.at[x, z], gat.at[x, z], gz_ss, gz_rs, at(dz=oz))
+    later(gat.at[0, pl.ds(0, 7)], gz_ss)
     wait_bytes(gat.at[x, pl.ds(0, 7)], gz_rs)
     for ox in FAR_X:
         send(gat.at[x], gat.at[x], gx_ss, gx_rs.at[ox - 1], at(dx=ox))
+    later(gat.at[pl.ds(0, 3)], gx_ss)
 
     def widen(xx):
         block = gat[xx].reshape(128, WIDTH).astype(F32)
-        act_v[xx] = (block * gain_ref[...]).astype(BF16)
+        act_v[xx] = (block * gain_ref[...].reshape(1, WIDTH)).astype(BF16)
         square = block * block
         high = square.astype(BF16)
         low = (square - high.astype(F32)).astype(BF16)
@@ -331,31 +363,26 @@
         widen(xx)
     for n, (oy, flip) in enumerate([(2, True), (2, False), (1, True), (3, True), (1, False), (3, False), (0, True)]):
         send(ssq_send, ssq_recv.at[n], ssq_ss, ssq_rs, at(dy=oy, flip=flip))
+    later(ssq_recv, ssq_ss)
 
     loads[4].wait()
     loads[5].wait()
 
     def products(half):
         act = act_v[pl.ds(half * 2, 2)].reshape(256, WIDTH)
-        return dot(act, wg_v[...]), dot(act, wu_v[...])
-
-    gate, up = products(1 - c)
-    gs_send[0] = gate.astype(BF16)
-    gs_send[1] = up.astype(BF16)
+        return dot_t(act, wgu_v[...])
+
+    gs_send[...] = products(1 - c).astype(BF16).reshape(NY, 64, 2 * FFD)
     send(gs_send, gs_recv, gs_ss, gs_rs, at(flip=True))
-    gate, up = products(c)
-    gs_own[0] = gate.reshape(NY, 64, FFD)
-    gs_own[1] = up.reshape(NY, 64, FFD)
+    later(gs_send, gs_ss)
+    gs_own[...] = products(c).reshape(NY, 64, 2 * FFD)
     wait_bytes(gs_recv, gs_rs)
     for oy in FAR_Y:
         yy = (y + oy) % NY
-        for k in range(2):
-            pair = gs_own[k, yy] + gs_recv[k, pl.ds(pl.multiple_of(yy * 64, 64), 64), :].astype(F32)
-            gy_send[oy - 1, k] = pair.astype(BF16)
+        gy_send[oy - 1] = (gs_own[yy] + gs_recv[yy].astype(F32)).astype(BF16)
         send(gy_send.at[oy - 1], gy_recv.at[oy - 1], gy_ss, gy_rs, at(dy=oy))
-    gate, up = (
-        gs_own[k, y] + gs_recv[k, pl.ds(pl.multiple_of(y * 64, 64), 64), :].astype(F32) for k in range(2)
-    )
+    later(gy_send, gy_ss)
+    both = gs_own[y] + gs_recv[y].astype(F32)
     wait_bytes(ssq_recv, ssq_rs)
     squares = ssq_send[...]
     for n in range(7):
@@ -370,15 +397,17 @@
     scale = lax.rsqrt(mean / D + EPSILON)
     wait_bytes(gy_recv, gy_rs)
     for n in range(3):
-        gate = gate + gy_recv[n, 0].astype(F32)
-        up = up + gy_recv[n, 1].astype(F32)
-    gate = gate * scale
-    hidden = (gate / (1.0 + jnp.exp(-gate)) * (up * scale)).astype(BF16)
+        both = both + gy_recv[n].astype(F32)
+    both = both * scale
+    gate, up = both[:, :FFD], both[:, FFD:]
+    hidden = (gate / (1.0 + jnp.exp(-gate)) * up).astype(BF16)
 
     hid[c, y] = hidden
     for oy in FAR_Y:
         send(hid.at[c, y], hid.at[c, y], hy_ss, hy_rs.at[oy - 1], at(dy=oy))
     send(hid.at[c, y], hid.at[c, y], hc_ss, hc_rs, at(flip=True))
+    later(hid.at[0, pl.ds(0, 3)], hy_ss)
+    later(hid.at[0], hc_ss)
     for oy in (1, 3, 2):
         yy = (y + NY - oy) % NY
         wait_bytes(hid.at[c, yy], hy_rs.at[oy - 1])
@@ -392,31 +421,8 @@
     )
     out_ref[...] = (stream_v[...].astype(F32) + lowered).astype(BF16)
 
-    wait_bytes(asked_v.at[pl.ds(1, 31)], req_ss)
-    wait_bytes(pg_send.at[pl.ds(1, 31)], pg_ss)
-    wait_bytes(keys.at[pl.ds(0, 3)], key_ss)
-    wait_bytes(keys.at[pl.ds(0, 4)], sib_ss)
-    wait_bytes(hd_in.at[pl.ds(0, 15)], hd_ss)
-
-    @pl.when(to_self == 0)
-    def _():
-        wait_bytes(hd_in.at[0], hd_ss)
-
-    for _ in range(3):
-        wait_bytes(own_block, hb_ss)
-    for _ in range(4):
-        wait_bytes(own_block, hs_ss)
-    wait_bytes(px_recv, px_ss)
-    wait_bytes(pz_recv, pz_ss)
-    wait_bytes(gat.at[x, pl.ds(0, 7)], gz_ss)
-    wait_bytes(gat.at[pl.ds(0, 3)], gx_ss)
-    wait_bytes(ssq_recv, ssq_ss)
-    wait_bytes(gs_send, gs_ss)
-    wait_bytes(gy_send, gy_ss)
-    wait_bytes(hid.at[0, pl.ds(0, 3)], hy_ss)
-    wait_bytes(hid.at[0], hc_ss)
-    wait_bytes(dx_recv, dx_ss)
-    wait_bytes(dz_recv, dz_ss)
+    for end in ends:
+        end()
 
 
 def per_device(
@@ -432,8 +438,8 @@
         V((NZ, REQ_D, WIDTH), F32), V((NZ, REQ_D, WIDTH), BF16), V((7, REQ_D, WIDTH), BF16), one, one,
     ]
     scratch = [
-        V((256, COLS), BF16), V((128, TOK, COLS), BF16), V((HEADS, KL, VH), BF16), V((512, WIDTH), BF16),
-        V((WIDTH, FFD), BF16), V((WIDTH, FFD), BF16), V((FFD, WIDTH), BF16), dma((7,)),
+        V((256, COLS), BF16), V((TOK, COLS, 128), BF16), V((128, TOK, COLS), BF16), V((HEADS, KL, VH), BF16),
+        V((512, WIDTH), BF16), V((2 * FFD, WIDTH), BF16), V((FFD, WIDTH), BF16), dma((7,)),
         V((1, 1, 128), I32), V((32, 1, 128), I32), pltpu.SMEM((32, 1, 128), I32),
         V((1, 1, 256), I32), pltpu.SMEM((1, 1, 256), I32), V((REQ_D, 256), F32), dma((2,)), one, one,
         V((32, 16, COLS), BF16), V((32, 16, COLS), BF16), one, one,
@@ -444,8 +450,8 @@
         *rs_scratch,
         V((REQ_D, WIDTH), BF16), V((NX, NZ, REQ_D, WIDTH), BF16), one, one, one, dma((3,)),
         V((NX, 128, WIDTH), BF16), V((NX, 8, 128), F32), V((7, NX, 8, 128), F32), one, one,
-        V((2, NY, 64, FFD), F32), V((2, 256, FFD), BF16), V((2, 256, FFD), BF16), one, one,
-        V((8, 128), F32), V((3, 2, 64, FFD), BF16), V((3, 2, 64, FFD), BF16), one, one,
+        V((NY, 64, 2 * FFD), F32), V((NY, 64, 2 * FFD), BF16), V((NY, 64, 2 * FFD), BF16), one, one,
+        V((3, 64, 2 * FFD), BF16), V((3, 64, 2 * FFD), BF16), one, one,
         V((NC, NY, 64, FFD), BF16), one, dma((3,)), one, one,
         *rs_scratch,
     ]
@@ -460,9 +466,9 @@
         ),
         name="layer",
     )(
-        page_owner, page_slot, lengths.reshape(1, REQ_D), resumed.reshape(1, REQ_D), new_latent, residual,
-        norm_gain.reshape(1, WIDTH), queries.reshape(256, COLS), pool, value_up, out_proj,
-        gate_weight, up_weight, down_weight,
+        page_owner.T, page_slot.T, lengths.reshape(1, REQ_D), resumed.reshape(1, REQ_D), new_latent, residual,
+        norm_gain, queries.reshape(256, COLS), pool.transpose(1, 2, 0), value_up, out_proj,
+        gate_weight.T, up_weight.T, down_weight,
     )
 
 

time: 162 us -> 151 us (0.932)
  local copies, waits for them, and re-layouts: 11.2 us -> 1.36 us
    unnamed x10 -> x1, local copies, waits for them, and re-layouts: 9.86 us -> 1.36 us
where the time goes in v2:
time: 151 us
  Pallas kernels  150 us (99%)
    pallas_call x1, Pallas kernels, per_device(): pl.pallas_call(kernel, out_shape=jax.ShapeDtypeStruct((REQ_D, WIDTH), BF1...  150 us

profile of v2, /device:TPU:1, one launch (start us, length us, event | category | flops | bytes accessed | tf_op | source)
XLA Modules:
  0.0 151.2 jit_solution(5680385203142943222)
XLA Ops:
  0.0 149.9 %layer.1 = bf16[16,896]{1,0:T(8,128)(2,1)} custom-call(s32[4,16]{1,0:T(4,128)} %bitcast.12, s32[4,16]{1,0:T(4,128)} %bitcast.13, s32[1,16]{1,0:T(1,128)} %bitcast.14, s32[1,16]{1,0:T(1,128)} %bitcast.15, bf16[16,576]{1,0:T(8,128)(2,1)} %nl_ref.1, bf16[16,896]{1,0:T(8,128)(2,1)} %resid_ref.1, f32[896]{0:T(1024)} %gain_ref.1, bf16[256,576]{1,0:T(8,128)(2,1)} %bitcast.11, ...), custom_call_target="tpu_custom_call" | custom-call | tf_op jit(solution)/shard_map/layer/pallas_call | solution.py:458
  149.9 1.4 copy.16

commit v3 on v2

--- a/solution.py
+++ b/solution.py
@@ -21,6 +21,8 @@
 PAGES = 4
 USED = 32
 WIDTH = 896
+WA, WB = 512, 384
+PARTS = ((0, 256), (256, 256), (512, 64))
 FFD = 576
 D = 7168
 SCORE_SCALE = 192.0 ** (-0.5)
@@ -76,13 +78,12 @@
     qt_v, scores_v,
     hd_send, hd_in, hd_ss, hd_rs,
     hb, hb_ss, hb_rs, hs_ss, hs_rs,
-    px_send, px_recv, px_ss, px_rs, pz_own, pz_send, pz_recv, pz_ss, pz_rs,
-    stream_v, gat, gz_ss, gz_rs, gx_ss, gx_rs,
+    sums,
+    gat_a, ga_ss, ga_rs, gax_ss, gax_rs, gat_b, gb_ss, gb_rs, gbz_ss, gbz_rs,
     act_v, ssq_send, ssq_recv, ssq_ss, ssq_rs,
     gs_own, gs_send, gs_recv, gs_ss, gs_rs,
     gy_send, gy_recv, gy_ss, gy_rs,
     hid, hy_ss, hy_rs, hc_ss, hc_rs,
-    dx_send, dx_recv, dx_ss, dx_rs, dz_own, dz_send, dz_recv, dz_ss, dz_rs,
 ):
     dp, tp = lax.axis_index("dp"), lax.axis_index("tp")
     x, z = dp // NZ, dp % NZ
@@ -202,56 +203,67 @@
     asked_copy.start()
     asked_copy.wait()
 
-    def gather(n_in, buffer, n_out):
-        pair = [pool_v[jnp.clip(asked_s[n_in, 0, 32 * k + dp], 0, 127)] for k in range(2)]
+    def gather(n_in, buffer, n_out, first, width):
+        pair = [
+            pool_v[jnp.clip(asked_s[n_in, 0, 32 * k + dp], 0, 127), :, first : first + width] for k in range(2)
+        ]
         buffer[n_out] = jnp.concatenate(pair, axis=0)
 
-    for ox, oz in FAR_DP:
-        n_out = ox * NZ + oz
-        gather(((NX - ox) % NX) * NZ + (NZ - oz) % NZ, pg_send, n_out)
-        send(pg_send.at[n_out], pg_recv.at[n_out], pg_ss, pg_rs, at(ox, oz))
-    later(pg_send.at[pl.ds(1, 31)], pg_ss)
-    gather(0, pg_recv, 0)
-    wait_bytes(pg_recv.at[pl.ds(1, 31)], pg_rs)
-
-    def pick(u, carry):
-        pair = []
-        for k in range(2):
-            source = jnp.clip(sel_s[0, 0, (2 * u + k) * TOK], 0, 63)
-            both = pg_recv[lax.shift_right_logical(source, 1)]
-            pair.append(jnp.where(jnp.bitwise_and(source, 1) == 1, both[TOK:], both[:TOK]))
-        keys[0, pl.ds(pl.multiple_of(u * 16, 16), 16), :] = jnp.concatenate(pair, axis=0)
-        return carry
-
-    lax.fori_loop(0, USED // 2, pick, 0)
-    for oy in FAR_Y:
-        send(keys.at[0], keys.at[oy], key_ss, key_rs.at[oy], at(dy=oy))
-    send(keys.at[0], keys.at[4], sib_ss, sib_rs.at[0], at(flip=True))
-    later(keys.at[pl.ds(0, 3)], key_ss)
-    later(keys.at[pl.ds(0, 4)], sib_ss)
-
-    qt = qt_v[...]
+    for i, (first, width) in enumerate(PARTS):
+        for ox, oz in FAR_DP:
+            n_out = ox * NZ + oz
+            gather(((NX - ox) % NX) * NZ + (NZ - oz) % NZ, pg_send[i], n_out, first, width)
+            send(pg_send[i].at[n_out], pg_recv[i].at[n_out], pg_ss.at[i], pg_rs.at[i], at(ox, oz))
+        later(pg_send[i].at[pl.ds(1, 31)], pg_ss.at[i])
+    for i, (first, width) in enumerate(PARTS):
+        gather(0, pg_recv[i], 0, first, width)
+
+    for i in range(3):
+        wait_bytes(pg_recv[i].at[pl.ds(1, 31)], pg_rs.at[i])
+
+        def pick(u, carry):
+            pair = []
+            for k in range(2):
+                source = jnp.clip(sel_s[0, 0, (2 * u + k) * TOK], 0, 63)
+                both = pg_recv[i][lax.shift_right_logical(source, 1)]
+                pair.append(jnp.where(jnp.bitwise_and(source, 1) == 1, both[TOK:], both[:TOK]))
+            keys[i][0, pl.ds(pl.multiple_of(u * 16, 16), 16), :] = jnp.concatenate(pair, axis=0)
+            return carry
+
+        lax.fori_loop(0, USED // 2, pick, 0)
+        for oy in FAR_Y:
+            send(keys[i].at[0], keys[i].at[oy], key_ss.at[i], key_rs.at[i, oy], at(dy=oy))
+        send(keys[i].at[0], keys[i].at[4], sib_ss.at[i], sib_rs.at[i, 0], at(flip=True))
+        later(keys[i].at[pl.ds(0, 3)], key_ss.at[i])
+        later(keys[i].at[pl.ds(0, 4)], sib_ss.at[i])
+
     limit = limit_v[...].reshape(1, REQ_D, USED * TOK)
     token = (lax.broadcasted_iota(I32, (1, 1, USED * TOK), 2) % TOK).astype(F32)
-
-    def score_block(n, source_tp):
-        block = (dot_t(qt, keys[n]) * SCORE_SCALE).reshape(HEADS, REQ_D, USED * TOK)
-        usable = limit > token + (source_tp * TOK).astype(F32)
-        block = jnp.where(usable, block, -jnp.inf)
-        scores_v[n] = block.reshape(256, USED * TOK)
 
     def source_of(n):
         core = c if n < 4 else 1 - c
         return ((y + NY - n % 4) % NY) * NC + core
 
-    score_block(0, source_of(0))
-    for oy in (1, 3, 2):
-        wait_bytes(keys.at[oy], key_rs.at[oy])
-        send(keys.at[oy], keys.at[4 + oy], sib_ss, sib_rs.at[oy], at(flip=True))
-        score_block(oy, source_of(oy))
-    for oy in (0, 1, 3, 2):
-        wait_bytes(keys.at[4 + oy], sib_rs.at[oy])
-        score_block(4 + oy, source_of(4 + oy))
+    def score_block(i, n):
+        first, width = PARTS[i]
+        block = dot_t(qt_v[:, first : first + width], keys[i][n])
+        if i:
+            block = scores_v[n] + block
+        if i == 2:
+            usable = limit > token + (source_of(n) * TOK).astype(F32)
+            block = (block * SCORE_SCALE).reshape(HEADS, REQ_D, USED * TOK)
+            block = jnp.where(usable, block, -jnp.inf).reshape(256, USED * TOK)
+        scores_v[n] = block
+
+    for i in range(3):
+        for oy in (1, 3, 2):
+            wait_bytes(keys[i].at[oy], key_rs.at[i, oy])
+            send(keys[i].at[oy], keys[i].at[4 + oy], sib_ss.at[i], sib_rs.at[i, oy], at(flip=True))
+        for n in range(4):
+            score_block(i, n)
+        for oy in (0, 1, 3, 2):
+            wait_bytes(keys[i].at[4 + oy], sib_rs.at[i, oy])
+            score_block(i, 4 + oy)
 
     peak = scores_v[0]
     for n in range(1, 8):
@@ -259,11 +271,13 @@
     top = jnp.maximum(own_score, jnp.max(peak, axis=1, keepdims=True))
     own_weight = jnp.exp(own_score - top)
     weight_lanes = jnp.zeros((256, USED * TOK), F32)
-    latent = jnp.zeros((256, KL), F32)
+    halves = [jnp.zeros((256, 256), F32)] * 2
     for n in range(8):
         weights = jnp.exp(scores_v[n] - top)
         weight_lanes = weight_lanes + weights
-        latent = latent + dot(weights.astype(BF16), keys[n, :, :KL])
+        weights = weights.astype(BF16)
+        halves = [half + dot(weights, keys[i][n]) for i, half in enumerate(halves)]
+    latent = jnp.concatenate(halves, axis=1)
     weight_sum = own_weight + jnp.sum(weight_lanes, axis=1, keepdims=True)
     own_latent = nl_ref[:, :KL].astype(F32).reshape(1, REQ_D, KL)
     latent = latent.reshape(HEADS, REQ_D, KL) + own_weight.reshape(HEADS, REQ_D, 1) * own_latent
@@ -309,58 +323,100 @@
     for oy in range(4):
         wait_bytes(own_block, hs_rs.at[oy])
 
-    def reduce_scatter(rows_of, weight, place, x_send, x_recv, x_ss, x_rs, z_own, z_send, z_recv, z_ss, z_rs):
+    def sum_over_dp(rows_x, rows_all, weight, place, bufs, ready_a, ready_b):
+        (a_send, a_recv, a_ss, a_rs, a_own, a_mid, am_recv, am_ss, am_rs,
+         b_send, b_recv, b_ss, b_rs, b_own, b_mid, bm_recv, bm_ss, bm_rs) = bufs
         for ox in FAR_X:
-            x_send[ox - 1] = dot(rows_of((x + ox) % NX), weight).astype(BF16)
-            send(x_send.at[ox - 1], x_recv.at[ox - 1], x_ss, x_rs, at(dx=ox))
-        later(x_send, x_ss)
-        total = dot(rows_of(x), weight)
-        wait_bytes(x_recv, x_rs)
+            a_send[ox - 1] = dot(rows_x((x + ox) % NX), weight[:, :WA]).astype(BF16)
+            send(a_send.at[ox - 1], a_recv.at[ox - 1], a_ss, a_rs, at(dx=ox))
+        later(a_send, a_ss)
+        b_send[...] = dot(rows_all(), weight[:, WA:]).astype(BF16).reshape(NX, NZ, REQ_D, WB)
+        for oz in FAR_Z:
+            send(b_send.at[:, place((z + oz) % NZ)], b_recv.at[oz - 1], b_ss, b_rs, at(dz=oz))
+        later(b_recv, b_ss)
+        total = dot(rows_x(x), weight[:, :WA])
+        wait_bytes(a_recv, a_rs)
         for n in range(3):
-            total = total + x_recv[n].astype(F32)
-        total = total.reshape(NZ, REQ_D, WIDTH)
-        z_own[...] = total
-        z_send[...] = total.astype(BF16)
+            total = total + a_recv[n].astype(F32)
+        total = total.reshape(NZ, REQ_D, WA)
+        a_own[...] = total
+        a_mid[...] = total.astype(BF16)
         for oz in FAR_Z:
-            send(z_send.at[place((z + oz) % NZ)], z_recv.at[oz - 1], z_ss, z_rs, at(dz=oz))
-        later(z_recv, z_ss)
-        mine = z_own[place(z)]
-        wait_bytes(z_recv, z_rs)
+            send(a_mid.at[place((z + oz) % NZ)], am_recv.at[oz - 1], am_ss, am_rs, at(dz=oz))
+        later(am_recv, am_ss)
+        total = b_send[:, place(z)].astype(F32)
+        wait_bytes(b_recv, b_rs)
         for n in range(7):
-            mine = mine + z_recv[n].astype(F32)
-        return mine
+            total = total + b_recv[n].astype(F32)
+        b_own[...] = total
+        b_mid[...] = total.astype(BF16)
+        for ox in FAR_X:
+            send(b_mid.at[(x + ox) % NX], bm_recv.at[ox - 1], bm_ss, bm_rs, at(dx=ox))
+        later(bm_recv, bm_ss)
+        mine = a_own[place(z)]
+        wait_bytes(am_recv, am_rs)
+        for n in range(7):
+            mine = mine + am_recv[n].astype(F32)
+        ready_a(mine)
+        mine = b_own[x]
+        wait_bytes(bm_recv, bm_rs)
+        for n in range(3):
+            mine = mine + bm_recv[n].astype(F32)
+        ready_b(mine)
+
+    def stream_a(attended):
+        stream = (resid_ref[:, :WA].astype(F32) + attended).astype(BF16)
+        gat_a[x, z] = stream
+        for oz in FAR_Z:
+            send(gat_a.at[x, z], gat_a.at[x, z], ga_ss, ga_rs, at(dz=oz))
+        later(gat_a.at[0, pl.ds(0, 7)], ga_ss)
+
+    def stream_b(attended):
+        stream = (resid_ref[:, WA:].astype(F32) + attended).astype(BF16)
+        gat_b[x, z] = stream
+        for ox in FAR_X:
+            send(gat_b.at[x, z], gat_b.at[x, z], gb_ss, gb_rs, at(dx=ox))
+        later(gat_b.at[0, pl.ds(0, 3)], gb_ss)
 
     loads[3].wait()
-    attended = reduce_scatter(
-        lambda xx: hb[xx].reshape(128, 512), wo_v[...], lambda zz: (zz % 2) * 4 + zz // 2,
-        px_send, px_recv, px_ss, px_rs, pz_own, pz_send, pz_recv, pz_ss, pz_rs,
+    sum_over_dp(
+        lambda xx: hb[xx].reshape(128, 512), lambda: hb[...].reshape(512, 512), wo_v,
+        lambda zz: (zz % 2) * 4 + zz // 2, sums[0], stream_a, stream_b,
     )
-    stream = (resid_ref[...].astype(F32) + attended).astype(BF16)
-    stream_v[...] = stream
-
-    gat[x, z] = stream
+    wait_bytes(gat_a.at[0, pl.ds(0, 7)], ga_rs)
+    for ox in FAR_X:
+        send(gat_a.at[x], gat_a.at[x], gax_ss, gax_rs.at[ox - 1], at(dx=ox))
+    later(gat_a.at[pl.ds(0, 3)], gax_ss)
+    wait_bytes(gat_b.at[0, pl.ds(0, 3)], gb_rs)
     for oz in FAR_Z:
-        send(gat.at[x, z], gat.at[x, z], gz_ss, gz_rs, at(dz=oz))
-    later(gat.at[0, pl.ds(0, 7)], gz_ss)
-    wait_bytes(gat.at[x, pl.ds(0, 7)], gz_rs)
-    for ox in FAR_X:
-        send(gat.at[x], gat.at[x], gx_ss, gx_rs.at[ox - 1], at(dx=ox))
-    later(gat.at[pl.ds(0, 3)], gx_ss)
-
-    def widen(xx):
-        block = gat[xx].reshape(128, WIDTH).astype(F32)
-        act_v[xx] = (block * gain_ref[...].reshape(1, WIDTH)).astype(BF16)
+        send(gat_b.at[:, z], gat_b.at[:, z], gbz_ss, gbz_rs, at(dz=oz))
+    later(gat_b.at[:, pl.ds(0, 7)], gbz_ss)
+
+    def widen(block, gain):
+        block = block.astype(F32)
         square = block * block
         high = square.astype(BF16)
         low = (square - high.astype(F32)).astype(BF16)
-        ones = jnp.ones((8, WIDTH), BF16)
-        ssq_send[xx] = dot_t(ones, high) + dot_t(ones, low)
-
-    widen(x)
+        ones = jnp.ones((8, block.shape[1]), BF16)
+        return (block * gain).astype(BF16), (dot_t(ones, high) + dot_t(ones, low))[0:1]
+
+    gain = gain_ref[...].reshape(1, WIDTH)
+
+    def widen_a(xx):
+        act, squares = widen(gat_a[xx].reshape(128, WA), gain[:, :WA])
+        act_v[pl.ds(xx * 2, 2), :, :WA] = act.reshape(2, 64, WA)
+        ssq_send[xx] = squares
+
+    widen_a(x)
     for ox in (1, 3, 2):
         xx = (x + NX - ox) % NX
-        wait_bytes(gat.at[xx], gx_rs.at[ox - 1])
-        widen(xx)
+        wait_bytes(gat_a.at[xx], gax_rs.at[ox - 1])
+        widen_a(xx)
+    wait_bytes(gat_b.at[:, pl.ds(0, 7)], gbz_rs)
+    for xx in range(NX):
+        act, squares = widen(gat_b[xx].reshape(128, WB), gain[:, WA:])
+        act_v[2 * xx : 2 * xx + 2, :, WA:] = act.reshape(2, 64, WB)
+        ssq_send[xx] = ssq_send[xx] + squares
     for n, (oy, flip) in enumerate([(2, True), (2, False), (1, True), (3, True), (1, False), (3, False), (0, True)]):
         send(ssq_send, ssq_recv.at[n], ssq_ss, ssq_rs, at(dy=oy, flip=flip))
     later(ssq_recv, ssq_ss)
@@ -368,21 +424,28 @@
     loads[4].wait()
     loads[5].wait()
 
-    def products(half):
-        act = act_v[pl.ds(half * 2, 2)].reshape(256, WIDTH)
-        return dot_t(act, wgu_v[...])
-
-    gs_send[...] = products(1 - c).astype(BF16).reshape(NY, 64, 2 * FFD)
-    send(gs_send, gs_recv, gs_ss, gs_rs, at(flip=True))
+    def products(half, pair):
+        act = jnp.concatenate([act_v[half * 4 + (y + oy) % NY] for oy in pair], axis=0)
+        return dot_t(act, wgu_v[...]).reshape(2, 64, 2 * FFD)
+
+    def to_core(k, pair):
+        gs_send[k] = products(1 - c, pair).astype(BF16)
+        send(gs_send.at[k], gs_recv.at[k], gs_ss, gs_rs.at[k], at(flip=True))
+
+    pairs = ((2, 1), (3, 0))
+    to_core(0, pairs[0])
+    gs_own[0] = products(c, pairs[0])
+    to_core(1, pairs[1])
     later(gs_send, gs_ss)
-    gs_own[...] = products(c).reshape(NY, 64, 2 * FFD)
-    wait_bytes(gs_recv, gs_rs)
-    for oy in FAR_Y:
-        yy = (y + oy) % NY
-        gy_send[oy - 1] = (gs_own[yy] + gs_recv[yy].astype(F32)).astype(BF16)
-        send(gy_send.at[oy - 1], gy_recv.at[oy - 1], gy_ss, gy_rs, at(dy=oy))
+    gs_own[1] = products(c, pairs[1])
+    for k, pair in enumerate(pairs):
+        wait_bytes(gs_recv.at[k], gs_rs.at[k])
+        for n, oy in enumerate(pair):
+            both = gs_own[k, n] + gs_recv[k, n].astype(F32)
+            if oy:
+                gy_send[oy - 1] = both.astype(BF16)
+                send(gy_send.at[oy - 1], gy_recv.at[oy - 1], gy_ss, gy_rs, at(dy=oy))
     later(gy_send, gy_ss)
-    both = gs_own[y] + gs_recv[y].astype(F32)
     wait_bytes(ssq_recv, ssq_rs)
     squares = ssq_send[...]
     for n in range(7):
@@ -392,7 +455,7 @@
     mean = jnp.zeros((64, 1), F32)
     for n in range(NX):
         mean = mean + jnp.sum(
-            jnp.where(row_id == lane_id + 128 * n, squares[n, 0:1, :], 0.0), axis=1, keepdims=True
+            jnp.where(row_id == lane_id + 128 * n, squares[n], 0.0), axis=1, keepdims=True
         )
     scale = lax.rsqrt(mean / D + EPSILON)
     wait_bytes(gy_recv, gy_rs)
@@ -415,12 +478,17 @@
     wait_bytes(hid.at[1 - c], hc_rs)
 
     loads[6].wait()
-    lowered = reduce_scatter(
-        lambda xx: hid[xx // 2, pl.ds((xx % 2) * 2, 2)].reshape(128, FFD), wd_v[...], lambda zz: zz,
-        dx_send, dx_recv, dx_ss, dx_rs, dz_own, dz_send, dz_recv, dz_ss, dz_rs,
+
+    def out_a(lowered):
+        out_ref[:, :WA] = (gat_a[x, z].astype(F32) + lowered).astype(BF16)
+
+    def out_b(lowered):
+        out_ref[:, WA:] = (gat_b[x, z].astype(F32) + lowered).astype(BF16)
+
+    sum_over_dp(
+        lambda xx: hid[xx // 2, pl.ds((xx % 2) * 2, 2)].reshape(128, FFD), lambda: hid[...].reshape(512, FFD), wd_v,
+        lambda zz: zz, sums[1], out_a, out_b,
     )
-    out_ref[...] = (stream_v[...].astype(F32) + lowered).astype(BF16)
-
     for end in ends:
         end()
 
@@ -433,27 +501,29 @@
     anywhere = pl.BlockSpec(memory_space=pl.ANY)
     dma, V = pltpu.SemaphoreType.DMA, pltpu.VMEM
     one = dma
-    rs_scratch = [
-        V((3, 128, WIDTH), BF16), V((3, 128, WIDTH), BF16), one, one,
-        V((NZ, REQ_D, WIDTH), F32), V((NZ, REQ_D, WIDTH), BF16), V((7, REQ_D, WIDTH), BF16), one, one,
+    sum_scratch = [
+        V((3, 128, WA), BF16), V((3, 128, WA), BF16), one, one,
+        V((NZ, REQ_D, WA), F32), V((NZ, REQ_D, WA), BF16), V((7, REQ_D, WA), BF16), one, one,
+        V((NX, NZ, REQ_D, WB), BF16), V((7, NX, REQ_D, WB), BF16), one, one,
+        V((NX, REQ_D, WB), F32), V((NX, REQ_D, WB), BF16), V((3, REQ_D, WB), BF16), one, one,
     ]
     scratch = [
         V((256, COLS), BF16), V((TOK, COLS, 128), BF16), V((128, TOK, COLS), BF16), V((HEADS, KL, VH), BF16),
         V((512, WIDTH), BF16), V((2 * FFD, WIDTH), BF16), V((FFD, WIDTH), BF16), dma((7,)),
         V((1, 1, 128), I32), V((32, 1, 128), I32), pltpu.SMEM((32, 1, 128), I32),
         V((1, 1, 256), I32), pltpu.SMEM((1, 1, 256), I32), V((REQ_D, 256), F32), dma((2,)), one, one,
-        V((32, 16, COLS), BF16), V((32, 16, COLS), BF16), one, one,
-        V((8, 256, COLS), BF16), one, dma((4,)), one, dma((4,)),
+        [V((32, 16, w), BF16) for _, w in PARTS], [V((32, 16, w), BF16) for _, w in PARTS], dma((3,)), dma((3,)),
+        [V((8, 256, w), BF16) for _, w in PARTS], dma((3,)), dma((3, 4)), dma((3,)), dma((3, 4)),
         V((256, COLS), BF16), V((8, 256, 256), F32),
         V((HEADS, 16, VH), BF16), V((16, 16, VH), BF16), one, one,
         V((NX, NC, 64, 512), BF16), one, dma((4,)), one, dma((4,)),
-        *rs_scratch,
-        V((REQ_D, WIDTH), BF16), V((NX, NZ, REQ_D, WIDTH), BF16), one, one, one, dma((3,)),
-        V((NX, 128, WIDTH), BF16), V((NX, 8, 128), F32), V((7, NX, 8, 128), F32), one, one,
-        V((NY, 64, 2 * FFD), F32), V((NY, 64, 2 * FFD), BF16), V((NY, 64, 2 * FFD), BF16), one, one,
+        [sum_scratch, sum_scratch],
+        V((NX, NZ, REQ_D, WA), BF16), one, one, one, dma((3,)),
+        V((NX, NZ, REQ_D, WB), BF16), one, one, one, one,
+        V((8, 64, WIDTH), BF16), V((NX, 1, 128), F32), V((7, NX, 1, 128), F32), one, one,
+        V((2, 2, 64, 2 * FFD), F32), V((2, 2, 64, 2 * FFD), BF16), V((2, 2, 64, 2 * FFD), BF16), one, dma((2,)),
         V((3, 64, 2 * FFD), BF16), V((3, 64, 2 * FFD), BF16), one, one,
         V((NC, NY, 64, FFD), BF16), one, dma((3,)), one, one,
-        *rs_scratch,
     ]
     return pl.pallas_call(
         kernel,

time: 151 us -> 129 us (0.85)
  Pallas kernels: 150 us -> 128 us
    pallas_call x1, Pallas kernels: 150 us -> 128 us  [per_device(): pl.pallas_call(kernel, out_shape=jax.ShapeDtypeStruct((REQ_D, WIDTH), BF1...]
where the time goes in v3:
time: 129 us
  Pallas kernels  128 us (99%)
  local copies, waits for them, and re-layouts  1.36 us (1%)
    pallas_call x1, Pallas kernels, per_device(): pl.pallas_call(kernel, out_shape=jax.ShapeDtypeStruct((REQ_D, WIDTH), BF1...  128 us

profile of v3, /device:TPU:1, one launch (start us, length us, event | category | flops | bytes accessed | tf_op | source)
XLA Modules:
  0.0 129.2 jit_solution(11912833805455370016)
XLA Ops:
  0.0 127.8 %layer.1 = bf16[16,896]{1,0:T(8,128)(2,1)} custom-call(s32[4,16]{1,0:T(4,128)} %bitcast.12, s32[4,16]{1,0:T(4,128)} %bitcast.13, s32[1,16]{1,0:T(1,128)} %bitcast.14, s32[1,16]{1,0:T(1,128)} %bitcast.15, bf16[16,576]{1,0:T(8,128)(2,1)} %nl_ref.1, bf16[16,896]{1,0:T(8,128)(2,1)} %resid_ref.1, f32[896]{0:T(1024)} %gain_ref.1, bf16[256,576]{1,0:T(8,128)(2,1)} %bitcast.11, ...), custom_call_target="tpu_custom_call" | custom-call | tf_op jit(solution)/shard_map/layer/pallas_call | solution.py:528
  127.8 1.4 %copy.16 = bf16[16,896]{1,0:T(8,128)(2,1)} copy(bf16[16,896]{1,0:T(8,128)(2,1)} %layer.1) | data formatting | bytes 57344

commit v4 on v3

--- a/solution.py
+++ b/solution.py
@@ -21,7 +21,8 @@
 PAGES = 4
 USED = 32
 WIDTH = 896
-WA, WB = 512, 384
+PARTS_A, FIRST_B = ((0, 384), (384, 256)), 640
+WB = WIDTH - FIRST_B
 PARTS = ((0, 256), (256, 256), (512, 64))
 FFD = 576
 D = 7168
@@ -71,7 +72,7 @@
     owner_ref, slot_ref, len_ref, res_ref, nl_ref, resid_ref, gain_ref,
     q_hbm, pool_hbm, vup_hbm, wo_hbm, wg_hbm, wu_hbm, wd_hbm,
     out_ref,
-    q_v, pool_t, pool_v, vup_v, wo_v, wgu_v, wd_v, load_sem,
+    q_v, pool_t, pool_v, vup_v, wo_v, wgu_v, wt_v, wd_v, load_sem,
     want_v, asked_v, asked_s, sel_v, sel_s, limit_v, smem_sem, req_ss, req_rs,
     pg_send, pg_recv, pg_ss, pg_rs,
     keys, key_ss, key_rs, sib_ss, sib_rs,
@@ -79,7 +80,7 @@
     hd_send, hd_in, hd_ss, hd_rs,
     hb, hb_ss, hb_rs, hs_ss, hs_rs,
     sums,
-    gat_a, ga_ss, ga_rs, gax_ss, gax_rs, gat_b, gb_ss, gb_rs, gbz_ss, gbz_rs,
+    gat_a, gat_b, gbz_ss, gbz_rs, resid_b, rb_ss, rb_rs,
     act_v, ssq_send, ssq_recv, ssq_ss, ssq_rs,
     gs_own, gs_send, gs_recv, gs_ss, gs_rs,
     gy_send, gy_recv, gy_ss, gy_rs,
@@ -179,6 +180,11 @@
         send(want_v.at[0], asked_v.at[ox * NZ + oz], req_ss, req_rs, at(ox, oz))
     later(asked_v.at[pl.ds(1, 31)], req_ss)
 
+    resid_b[pl.ds(x, 1)] = resid_ref[:, FIRST_B:].reshape(1, REQ_D, WB)
+    for ox in FAR_X:
+        send(resid_b.at[x], resid_b.at[x], rb_ss, rb_rs, at(dx=ox))
+    later(resid_b.at[pl.ds(0, 3)], rb_ss)
+
     loads[1].wait()
     rows = lax.broadcasted_iota(I32, (256, 256), 0)
     lanes = lax.broadcasted_iota(I32, (256, 256), 1)
@@ -218,7 +224,23 @@
     for i, (first, width) in enumerate(PARTS):
         gather(0, pg_recv[i], 0, first, width)
 
-    for i in range(3):
+    loads[4].wait()
+    loads[5].wait()
+    same = lax.broadcasted_iota(I32, (128, 128), 0) == lax.broadcasted_iota(I32, (128, 128), 1)
+    same = jnp.where(same, 1.0, 0.0).astype(BF16)
+    for first in range(0, WIDTH, 128):
+        wt_v[first : first + 128] = dot_t(same, wgu_v[:, first : first + 128]).astype(BF16)
+
+    def pass_on(i):
+        upper, lower = pl.ds(0, 128), pl.ds(128, 128)
+        wait_bytes(keys[i].at[1], key_rs.at[i, 1])
+        send(keys[i].at[1, upper], keys[i].at[2, upper], key_ss.at[i], key_rs.at[i, 2], at(dy=1))
+        send(keys[i].at[1], keys[i].at[5], sib_ss.at[i], sib_rs.at[i, 1], at(flip=True))
+        wait_bytes(keys[i].at[3], key_rs.at[i, 3])
+        send(keys[i].at[3, lower], keys[i].at[2, lower], key_ss.at[i], key_rs.at[i, 0], at(dy=3))
+        send(keys[i].at[3], keys[i].at[7], sib_ss.at[i], sib_rs.at[i, 3], at(flip=True))
+
+    for i in range(len(PARTS)):
         wait_bytes(pg_recv[i].at[pl.ds(1, 31)], pg_rs.at[i])
 
         def pick(u, carry):
@@ -231,11 +253,13 @@
             return carry
 
         lax.fori_loop(0, USED // 2, pick, 0)
-        for oy in FAR_Y:
+        for oy in FAR_Y if i == len(PARTS) - 1 else (1, 3):
             send(keys[i].at[0], keys[i].at[oy], key_ss.at[i], key_rs.at[i, oy], at(dy=oy))
         send(keys[i].at[0], keys[i].at[4], sib_ss.at[i], sib_rs.at[i, 0], at(flip=True))
         later(keys[i].at[pl.ds(0, 3)], key_ss.at[i])
         later(keys[i].at[pl.ds(0, 4)], sib_ss.at[i])
+        if i:
+            pass_on(i - 1)
 
     limit = limit_v[...].reshape(1, REQ_D, USED * TOK)
     token = (lax.broadcasted_iota(I32, (1, 1, USED * TOK), 2) % TOK).astype(F32)
@@ -249,16 +273,21 @@
         block = dot_t(qt_v[:, first : first + width], keys[i][n])
         if i:
             block = scores_v[n] + block
-        if i == 2:
+        if i == len(PARTS) - 1:
             usable = limit > token + (source_of(n) * TOK).astype(F32)
             block = (block * SCORE_SCALE).reshape(HEADS, REQ_D, USED * TOK)
             block = jnp.where(usable, block, -jnp.inf).reshape(256, USED * TOK)
         scores_v[n] = block
 
-    for i in range(3):
-        for oy in (1, 3, 2):
-            wait_bytes(keys[i].at[oy], key_rs.at[i, oy])
-            send(keys[i].at[oy], keys[i].at[4 + oy], sib_ss.at[i], sib_rs.at[i, oy], at(flip=True))
+    for i in range(len(PARTS)):
+        if i < len(PARTS) - 1:
+            wait_bytes(keys[i].at[2, pl.ds(0, 128)], key_rs.at[i, 2])
+            wait_bytes(keys[i].at[2, pl.ds(128, 128)], key_rs.at[i, 0])
+            send(keys[i].at[2], keys[i].at[6], sib_ss.at[i], sib_rs.at[i, 2], at(flip=True))
+        else:
+            for oy in (1, 3, 2):
+                wait_bytes(keys[i].at[oy], key_rs.at[i, oy])
+                send(keys[i].at[oy], keys[i].at[4 + oy], sib_ss.at[i], sib_rs.at[i, oy], at(flip=True))
         for n in range(4):
             score_block(i, n)
         for oy in (0, 1, 3, 2):
@@ -271,13 +300,13 @@
     top = jnp.maximum(own_score, jnp.max(peak, axis=1, keepdims=True))
     own_weight = jnp.exp(own_score - top)
     weight_lanes = jnp.zeros((256, USED * TOK), F32)
-    halves = [jnp.zeros((256, 256), F32)] * 2
+    pieces = [jnp.zeros((256, width), F32) for _, width in PARTS[:-1]]
     for n in range(8):
         weights = jnp.exp(scores_v[n] - top)
         weight_lanes = weight_lanes + weights
         weights = weights.astype(BF16)
-        halves = [half + dot(weights, keys[i][n]) for i, half in enumerate(halves)]
-    latent = jnp.concatenate(halves, axis=1)
+        pieces = [piece + dot(weights, keys[i][n]) for i, piece in enumerate(pieces)]
+    latent = jnp.concatenate(pieces, axis=1)
     weight_sum = own_weight + jnp.sum(weight_lanes, axis=1, keepdims=True)
     own_latent = nl_ref[:, :KL].astype(F32).reshape(1, REQ_D, KL)
     latent = latent.reshape(HEADS, REQ_D, KL) + own_weight.reshape(HEADS, REQ_D, 1) * own_latent
@@ -323,74 +352,87 @@
     for oy in range(4):
         wait_bytes(own_block, hs_rs.at[oy])
 
-    def sum_over_dp(rows_x, rows_all, weight, place, bufs, ready_a, ready_b):
-        (a_send, a_recv, a_ss, a_rs, a_own, a_mid, am_recv, am_ss, am_rs,
-         b_send, b_recv, b_ss, b_rs, b_own, b_mid, bm_recv, bm_ss, bm_rs) = bufs
-        for ox in FAR_X:
-            a_send[ox - 1] = dot(rows_x((x + ox) % NX), weight[:, :WA]).astype(BF16)
-            send(a_send.at[ox - 1], a_recv.at[ox - 1], a_ss, a_rs, at(dx=ox))
-        later(a_send, a_ss)
-        b_send[...] = dot(rows_all(), weight[:, WA:]).astype(BF16).reshape(NX, NZ, REQ_D, WB)
+    def sum_over_dp(rows_x, rows_all, weight, place, bufs, ready_a, gather_b, ready_b):
+        parts_a, (b_send, b_recv, b_ss, b_rs, b_own, b_mid, bm_recv, bm_ss, bm_rs) = bufs
+        for (first, width), (a_send, a_recv, a_ss, a_rs, *_) in zip(PARTS_A, parts_a):
+            for ox in FAR_X:
+                a_send[ox - 1] = dot(rows_x((x + ox) % NX), weight[:, first : first + width]).astype(BF16)
+                send(a_send.at[ox - 1], a_recv.at[ox - 1], a_ss, a_rs, at(dx=ox))
+            later(a_send, a_ss)
+        b_send[...] = dot(rows_all(), weight[:, FIRST_B:]).astype(BF16).reshape(NX, NZ, REQ_D, WB)
         for oz in FAR_Z:
             send(b_send.at[:, place((z + oz) % NZ)], b_recv.at[oz - 1], b_ss, b_rs, at(dz=oz))
         later(b_recv, b_ss)
-        total = dot(rows_x(x), weight[:, :WA])
-        wait_bytes(a_recv, a_rs)
-        for n in range(3):
-            total = total + a_recv[n].astype(F32)
-        total = total.reshape(NZ, REQ_D, WA)
-        a_own[...] = total
-        a_mid[...] = total.astype(BF16)
-        for oz in FAR_Z:
-            send(a_mid.at[place((z + oz) % NZ)], am_recv.at[oz - 1], am_ss, am_rs, at(dz=oz))
-        later(am_recv, am_ss)
+        own = dot(rows_x(x), weight[:, :FIRST_B])
+        for (first, width), (a_send, a_recv, a_ss, a_rs, a_own, a_mid, am_recv, am_ss, am_rs) in zip(PARTS_A, parts_a):
+            total = own[:, first : first + width]
+            wait_bytes(a_recv, a_rs)
+            for n in range(3):
+                total = total + a_recv[n].astype(F32)
+            total = total.reshape(NZ, REQ_D, width)
+            a_own[...] = total
+            a_mid[...] = total.astype(BF16)
+            for oz in FAR_Z:
+                send(a_mid.at[place((z + oz) % NZ)], am_recv.at[oz - 1], am_ss, am_rs, at(dz=oz))
+            later(am_recv, am_ss)
         total = b_send[:, place(z)].astype(F32)
         wait_bytes(b_recv, b_rs)
         for n in range(7):
             total = total + b_recv[n].astype(F32)
-        b_own[...] = total
-        b_mid[...] = total.astype(BF16)
-        for ox in FAR_X:
-            send(b_mid.at[(x + ox) % NX], bm_recv.at[ox - 1], bm_ss, bm_rs, at(dx=ox))
-        later(bm_recv, bm_ss)
-        mine = a_own[place(z)]
-        wait_bytes(am_recv, am_rs)
-        for n in range(7):
-            mine = mine + am_recv[n].astype(F32)
-        ready_a(mine)
-        mine = b_own[x]
-        wait_bytes(bm_recv, bm_rs)
-        for n in range(3):
-            mine = mine + bm_recv[n].astype(F32)
+        if gather_b:
+            bm_recv[x] = total.astype(BF16)
+            for ox in FAR_X:
+                send(bm_recv.at[x], bm_recv.at[x], bm_ss, bm_rs, at(dx=ox))
+            later(bm_recv.at[pl.ds(0, 3)], bm_ss)
+        else:
+            b_own[...] = total
+            b_mid[...] = total.astype(BF16)
+            for ox in FAR_X:
+                send(b_mid.at[(x + ox) % NX], bm_recv.at[ox - 1], bm_ss, bm_rs, at(dx=ox))
+            later(bm_recv, bm_ss)
+        for part, (_, _, _, _, a_own, _, am_recv, _, am_rs) in enumerate(parts_a):
+            mine = a_own[place(z)]
+            wait_bytes(am_recv, am_rs)
+            for n in range(7):
+                mine = mine + am_recv[n].astype(F32)
+            ready_a(part, mine)
+        if gather_b:
+            wait_bytes(bm_recv.at[pl.ds(0, 3)], bm_rs)
+            mine = bm_recv[0].astype(F32)
+            for n in range(1, NX):
+                mine = mine + bm_recv[n].astype(F32)
+        else:
+            mine = b_own[x]
+            wait_bytes(bm_recv, bm_rs)
+            for n in range(3):
+                mine = mine + bm_recv[n].astype(F32)
         ready_b(mine)
 
-    def stream_a(attended):
-        stream = (resid_ref[:, :WA].astype(F32) + attended).astype(BF16)
-        gat_a[x, z] = stream
+    def stream_a(part, attended):
+        first, width = PARTS_A[part]
+        gat, z_ss, z_rs, _, _ = gat_a[part]
+        gat[x, z] = (resid_ref[:, first : first + width].astype(F32) + attended).astype(BF16)
         for oz in FAR_Z:
-            send(gat_a.at[x, z], gat_a.at[x, z], ga_ss, ga_rs, at(dz=oz))
-        later(gat_a.at[0, pl.ds(0, 7)], ga_ss)
+            send(gat.at[x, z], gat.at[x, z], z_ss, z_rs, at(dz=oz))
+        later(gat.at[0, pl.ds(0, 7)], z_ss)
 
     def stream_b(attended):
-        stream = (resid_ref[:, WA:].astype(F32) + attended).astype(BF16)
-        gat_b[x, z] = stream
-        for ox in FAR_X:
-            send(gat_b.at[x, z], gat_b.at[x, z], gb_ss, gb_rs, at(dx=ox))
-        later(gat_b.at[0, pl.ds(0, 3)], gb_ss)
+        wait_bytes(resid_b.at[pl.ds(0, 3)], rb_rs)
+        gat_b[:, z] = (resid_b[...].astype(F32) + attended).astype(BF16)
+        for oz in FAR_Z:
+            send(gat_b.at[:, z], gat_b.at[:, z], gbz_ss, gbz_rs, at(dz=oz))
+        later(gat_b.at[:, pl.ds(0, 7)], gbz_ss)
 
     loads[3].wait()
     sum_over_dp(
         lambda xx: hb[xx].reshape(128, 512), lambda: hb[...].reshape(512, 512), wo_v,
-        lambda zz: (zz % 2) * 4 + zz // 2, sums[0], stream_a, stream_b,
+        lambda zz: (zz % 2) * 4 + zz // 2, sums[0], stream_a, True, stream_b,
     )
-    wait_bytes(gat_a.at[0, pl.ds(0, 7)], ga_rs)
-    for ox in FAR_X:
-        send(gat_a.at[x], gat_a.at[x], gax_ss, gax_rs.at[ox - 1], at(dx=ox))
-    later(gat_a.at[pl.ds(0, 3)], gax_ss)
-    wait_bytes(gat_b.at[0, pl.ds(0, 3)], gb_rs)
-    for oz in FAR_Z:
-        send(gat_b.at[:, z], gat_b.at[:, z], gbz_ss, gbz_rs, at(dz=oz))
-    later(gat_b.at[:, pl.ds(0, 7)], gbz_ss)
+    for gat, _, z_rs, x_ss, x_rs in gat_a:
+        wait_bytes(gat.at[0, pl.ds(0, 7)], z_rs)
+        for ox in FAR_X:
+            send(gat.at[x], gat.at[x], x_ss, x_rs.at[ox - 1], at(dx=ox))
+        later(gat.at[pl.ds(0, 3)], x_ss)
 
     def widen(block, gain):
         block = block.astype(F32)
@@ -402,31 +444,26 @@
 
     gain = gain_ref[...].reshape(1, WIDTH)
 
-    def widen_a(xx):
-        act, squares = widen(gat_a[xx].reshape(128, WA), gain[:, :WA])
-        act_v[pl.ds(xx * 2, 2), :, :WA] = act.reshape(2, 64, WA)
-        ssq_send[xx] = squares
-
-    widen_a(x)
-    for ox in (1, 3, 2):
-        xx = (x + NX - ox) % NX
-        wait_bytes(gat_a.at[xx], gax_rs.at[ox - 1])
-        widen_a(xx)
+    for part, ((first, width), (gat, _, _, _, x_rs)) in enumerate(zip(PARTS_A, gat_a)):
+        for ox in (0, 1, 3, 2):
+            xx = (x + NX - ox) % NX
+            if ox:
+                wait_bytes(gat.at[xx], x_rs.at[ox - 1])
+            act, squares = widen(gat[xx].reshape(128, width), gain[:, first : first + width])
+            act_v[pl.ds(xx * 2, 2), :, first : first + width] = act.reshape(2, 64, width)
+            ssq_send[xx] = ssq_send[xx] + squares if part else squares
     wait_bytes(gat_b.at[:, pl.ds(0, 7)], gbz_rs)
     for xx in range(NX):
-        act, squares = widen(gat_b[xx].reshape(128, WB), gain[:, WA:])
-        act_v[2 * xx : 2 * xx + 2, :, WA:] = act.reshape(2, 64, WB)
+        act, squares = widen(gat_b[xx].reshape(128, WB), gain[:, FIRST_B:])
+        act_v[2 * xx : 2 * xx + 2, :, FIRST_B:] = act.reshape(2, 64, WB)
         ssq_send[xx] = ssq_send[xx] + squares
     for n, (oy, flip) in enumerate([(2, True), (2, False), (1, True), (3, True), (1, False), (3, False), (0, True)]):
         send(ssq_send, ssq_recv.at[n], ssq_ss, ssq_rs, at(dy=oy, flip=flip))
     later(ssq_recv, ssq_ss)
 
-    loads[4].wait()
-    loads[5].wait()
-
     def products(half, pair):
         act = jnp.concatenate([act_v[half * 4 + (y + oy) % NY] for oy in pair], axis=0)
-        return dot_t(act, wgu_v[...]).reshape(2, 64, 2 * FFD)
+        return dot(act, wt_v[...]).reshape(2, 64, 2 * FFD)
 
     def to_core(k, pair):
         gs_send[k] = products(1 - c, pair).astype(BF16)
@@ -479,15 +516,16 @@
 
     loads[6].wait()
 
-    def out_a(lowered):
-        out_ref[:, :WA] = (gat_a[x, z].astype(F32) + lowered).astype(BF16)
+    def out_a(part, lowered):
+        first, width = PARTS_A[part]
+        out_ref[:, first : first + width] = (gat_a[part][0][x, z].astype(F32) + lowered).astype(BF16)
 
     def out_b(lowered):
-        out_ref[:, WA:] = (gat_b[x, z].astype(F32) + lowered).astype(BF16)
+        out_ref[:, FIRST_B:] = (gat_b[x, z].astype(F32) + lowered).astype(BF16)
 
     sum_over_dp(
         lambda xx: hid[xx // 2, pl.ds((xx % 2) * 2, 2)].reshape(128, FFD), lambda: hid[...].reshape(512, FFD), wd_v,
-        lambda zz: zz, sums[1], out_a, out_b,
+        lambda zz: zz, sums[1], out_a, False, out_b,
     )
     for end in ends:
         end()
@@ -500,26 +538,32 @@
     vmem = pl.BlockSpec(memory_space=pltpu.VMEM)
     anywhere = pl.BlockSpec(memory_space=pl.ANY)
     dma, V = pltpu.SemaphoreType.DMA, pltpu.VMEM
-    one = dma
-    sum_scratch = [
-        V((3, 128, WA), BF16), V((3, 128, WA), BF16), one, one,
-        V((NZ, REQ_D, WA), F32), V((NZ, REQ_D, WA), BF16), V((7, REQ_D, WA), BF16), one, one,
-        V((NX, NZ, REQ_D, WB), BF16), V((7, NX, REQ_D, WB), BF16), one, one,
-        V((NX, REQ_D, WB), F32), V((NX, REQ_D, WB), BF16), V((3, REQ_D, WB), BF16), one, one,
-    ]
+    one, n = dma, len(PARTS)
+    def sum_scratch(gather_b):
+        return [
+            [
+                [V((3, 128, w), BF16), V((3, 128, w), BF16), one, one,
+                 V((NZ, REQ_D, w), F32), V((NZ, REQ_D, w), BF16), V((7, REQ_D, w), BF16), one, one]
+                for _, w in PARTS_A
+            ],
+            [V((NX, NZ, REQ_D, WB), BF16), V((7, NX, REQ_D, WB), BF16), one, one,
+             V((NX, REQ_D, WB), F32), V((NX, REQ_D, WB), BF16),
+             V((NX, NX, REQ_D, WB) if gather_b else (3, REQ_D, WB), BF16), one, one],
+        ]
+
     scratch = [
         V((256, COLS), BF16), V((TOK, COLS, 128), BF16), V((128, TOK, COLS), BF16), V((HEADS, KL, VH), BF16),
-        V((512, WIDTH), BF16), V((2 * FFD, WIDTH), BF16), V((FFD, WIDTH), BF16), dma((7,)),
+        V((512, WIDTH), BF16), V((2 * FFD, WIDTH), BF16), V((WIDTH, 2 * FFD), BF16), V((FFD, WIDTH), BF16), dma((7,)),
         V((1, 1, 128), I32), V((32, 1, 128), I32), pltpu.SMEM((32, 1, 128), I32),
         V((1, 1, 256), I32), pltpu.SMEM((1, 1, 256), I32), V((REQ_D, 256), F32), dma((2,)), one, one,
-        [V((32, 16, w), BF16) for _, w in PARTS], [V((32, 16, w), BF16) for _, w in PARTS], dma((3,)), dma((3,)),
-        [V((8, 256, w), BF16) for _, w in PARTS], dma((3,)), dma((3, 4)), dma((3,)), dma((3, 4)),
+        [V((32, 16, w), BF16) for _, w in PARTS], [V((32, 16, w), BF16) for _, w in PARTS], dma((n,)), dma((n,)),
+        [V((8, 256, w), BF16) for _, w in PARTS], dma((n,)), dma((n, 4)), dma((n,)), dma((n, 4)),
         V((256, COLS), BF16), V((8, 256, 256), F32),
         V((HEADS, 16, VH), BF16), V((16, 16, VH), BF16), one, one,
         V((NX, NC, 64, 512), BF16), one, dma((4,)), one, dma((4,)),
-        [sum_scratch, sum_scratch],
-        V((NX, NZ, REQ_D, WA), BF16), one, one, one, dma((3,)),
-        V((NX, NZ, REQ_D, WB), BF16), one, one, one, one,
+        [sum_scratch(True), sum_scratch(False)],
+        [[V((NX, NZ, REQ_D, w), BF16), one, one, one, dma((3,))] for _, w in PARTS_A],
+        V((NX, NZ, REQ_D, WB), BF16), one, one, V((NX, REQ_D, WB), BF16), one, one,
         V((8, 64, WIDTH), BF16), V((NX, 1, 128), F32), V((7, NX, 1, 128), F32), one, one,
         V((2, 2, 64, 2 * FFD), F32), V((2, 2, 64, 2 * FFD), BF16), V((2, 2, 64, 2 * FFD), BF16), one, dma((2,)),
         V((3, 64, 2 * FFD), BF16), V((3, 64, 2 * FFD), BF16), one, one,

time: 129 us -> 123 us (0.953)
  Pallas kernels: 128 us -> 122 us
    pallas_call x1, Pallas kernels: 128 us -> 122 us  [per_device(): pl.pallas_call(kernel, out_shape=jax.ShapeDtypeStruct((REQ_D, WIDTH), BF1...]
where the time goes in v4:
time: 123 us
  Pallas kernels  122 us (99%)
  local copies, waits for them, and re-layouts  1.36 us (1%)
    pallas_call x1, Pallas kernels, per_device(): pl.pallas_call(kernel, out_shape=jax.ShapeDtypeStruct((REQ_D, WIDTH), BF1...  122 us

profile of v4, /device:TPU:1, one launch (start us, length us, event | category | flops | bytes accessed | tf_op | source)
XLA Modules:
  0.0 123.1 jit_solution(2960085966086152661)
XLA Ops:
  0.0 121.7 %layer.1 = bf16[16,896]{1,0:T(8,128)(2,1)} custom-call(s32[4,16]{1,0:T(4,128)} %bitcast.12, s32[4,16]{1,0:T(4,128)} %bitcast.13, s32[1,16]{1,0:T(1,128)} %bitcast.14, s32[1,16]{1,0:T(1,128)} %bitcast.15, bf16[16,576]{1,0:T(8,128)(2,1)} %nl_ref.1, bf16[16,896]{1,0:T(8,128)(2,1)} %resid_ref.1, f32[896]{0:T(1024)} %gain_ref.1, bf16[256,576]{1,0:T(8,128)(2,1)} %bitcast.11, ...), custom_call_target="tpu_custom_call" | custom-call | tf_op jit(solution)/shard_map/layer/pallas_call | solution.py:572
  121.7 1.4 %copy.16 = bf16[16,896]{1,0:T(8,128)(2,1)} copy(bf16[16,896]{1,0:T(8,128)(2,1)} %layer.1) | data formatting | bytes 57344

commit v5 on v4

--- a/solution.py
+++ b/solution.py
@@ -23,6 +23,7 @@
 WIDTH = 896
 PARTS_A, FIRST_B = ((0, 384), (384, 256)), 640
 WB = WIDTH - FIRST_B
+UNITS = ((0, 256), (256, 320))
 PARTS = ((0, 256), (256, 256), (512, 64))
 FFD = 576
 D = 7168
@@ -82,9 +83,7 @@
     sums,
     gat_a, gat_b, gbz_ss, gbz_rs, resid_b, rb_ss, rb_rs,
     act_v, ssq_send, ssq_recv, ssq_ss, ssq_rs,
-    gs_own, gs_send, gs_recv, gs_ss, gs_rs,
-    gy_send, gy_recv, gy_ss, gy_rs,
-    hid, hy_ss, hy_rs, hc_ss, hc_rs,
+    units, hids,
 ):
     dp, tp = lax.axis_index("dp"), lax.axis_index("tp")
     x, z = dp // NZ, dp % NZ
@@ -94,11 +93,15 @@
         core = 1 - c if flip else c
         return (((x + dx) % NX) * NZ + (z + dz) % NZ, ((y + dy) % NY) * NC + core)
 
+    unit_loads = [
+        (hbm.at[pl.ds(first, width)], wgu_v.at[pl.ds(2 * first + k * width, width)])
+        for first, width in UNITS
+        for k, hbm in enumerate((wg_hbm, wu_hbm))
+    ]
     loads = [
         pltpu.make_async_copy(src, dst, load_sem.at[i])
         for i, (src, dst) in enumerate(
-            [(pool_hbm, pool_t), (q_hbm, q_v), (vup_hbm, vup_v), (wo_hbm, wo_v),
-             (wg_hbm, wgu_v.at[pl.ds(0, FFD)]), (wu_hbm, wgu_v.at[pl.ds(FFD, FFD)]), (wd_hbm, wd_v)]
+            [(pool_hbm, pool_t), (q_hbm, q_v), (vup_hbm, vup_v), (wo_hbm, wo_v), (wd_hbm, wd_v), *unit_loads]
         )
     ]
     for load in loads:
@@ -224,8 +227,8 @@
     for i, (first, width) in enumerate(PARTS):
         gather(0, pg_recv[i], 0, first, width)
 
-    loads[4].wait()
-    loads[5].wait()
+    for load in loads[5:]:
+        load.wait()
     same = lax.broadcasted_iota(I32, (128, 128), 0) == lax.broadcasted_iota(I32, (128, 128), 1)
     same = jnp.where(same, 1.0, 0.0).astype(BF16)
     for first in range(0, WIDTH, 128):
@@ -461,28 +464,23 @@
         send(ssq_send, ssq_recv.at[n], ssq_ss, ssq_rs, at(dy=oy, flip=flip))
     later(ssq_recv, ssq_ss)
 
-    def products(half, pair):
-        act = jnp.concatenate([act_v[half * 4 + (y + oy) % NY] for oy in pair], axis=0)
-        return dot(act, wt_v[...]).reshape(2, 64, 2 * FFD)
-
-    def to_core(k, pair):
-        gs_send[k] = products(1 - c, pair).astype(BF16)
-        send(gs_send.at[k], gs_recv.at[k], gs_ss, gs_rs.at[k], at(flip=True))
-
-    pairs = ((2, 1), (3, 0))
-    to_core(0, pairs[0])
-    gs_own[0] = products(c, pairs[0])
-    to_core(1, pairs[1])
-    later(gs_send, gs_ss)
-    gs_own[1] = products(c, pairs[1])
-    for k, pair in enumerate(pairs):
-        wait_bytes(gs_recv.at[k], gs_rs.at[k])
-        for n, oy in enumerate(pair):
-            both = gs_own[k, n] + gs_recv[k, n].astype(F32)
-            if oy:
-                gy_send[oy - 1] = both.astype(BF16)
-                send(gy_send.at[oy - 1], gy_recv.at[oy - 1], gy_ss, gy_rs, at(dy=oy))
-    later(gy_send, gy_ss)
+    ways = (2, 1, 3, 0)
+
+    def products(half, part):
+        first, width = UNITS[part]
+        act = jnp.concatenate([act_v[half * 4 + (y + oy) % NY] for oy in ways], axis=0)
+        return dot(act, wt_v[:, 2 * first : 2 * (first + width)]).reshape(NY, 64, 2 * width)
+
+    for part, (own, to_core, from_core, core_ss, core_rs, to_y, from_y, y_ss, y_rs) in enumerate(units):
+        to_core[...] = products(1 - c, part).astype(BF16)
+        send(to_core, from_core, core_ss, core_rs, at(flip=True))
+        later(to_core, core_ss)
+        own[...] = products(c, part)
+        wait_bytes(from_core, core_rs)
+        for n in range(3):
+            to_y[n] = (own[n] + from_core[n].astype(F32)).astype(BF16)
+            send(to_y.at[n], from_y.at[n], y_ss, y_rs, at(dy=ways[n]))
+        later(to_y, y_ss)
     wait_bytes(ssq_recv, ssq_rs)
     squares = ssq_send[...]
     for n in range(7):
@@ -495,26 +493,30 @@
             jnp.where(row_id == lane_id + 128 * n, squares[n], 0.0), axis=1, keepdims=True
         )
     scale = lax.rsqrt(mean / D + EPSILON)
-    wait_bytes(gy_recv, gy_rs)
-    for n in range(3):
-        both = both + gy_recv[n].astype(F32)
-    both = both * scale
-    gate, up = both[:, :FFD], both[:, FFD:]
-    hidden = (gate / (1.0 + jnp.exp(-gate)) * up).astype(BF16)
-
-    hid[c, y] = hidden
-    for oy in FAR_Y:
-        send(hid.at[c, y], hid.at[c, y], hy_ss, hy_rs.at[oy - 1], at(dy=oy))
-    send(hid.at[c, y], hid.at[c, y], hc_ss, hc_rs, at(flip=True))
-    later(hid.at[0, pl.ds(0, 3)], hy_ss)
-    later(hid.at[0], hc_ss)
-    for oy in (1, 3, 2):
-        yy = (y + NY - oy) % NY
-        wait_bytes(hid.at[c, yy], hy_rs.at[oy - 1])
-        send(hid.at[c, yy], hid.at[c, yy], hc_ss, hc_rs, at(flip=True))
-    wait_bytes(hid.at[1 - c], hc_rs)
-
-    loads[6].wait()
+    for (_, width), (own, _, from_core, _, _, _, from_y, _, y_rs), (hid, hy_ss, hy_rs, hc_ss, hc_rs) in zip(
+        UNITS, units, hids
+    ):
+        both = own[3] + from_core[3].astype(F32)
+        wait_bytes(from_y, y_rs)
+        for n in range(3):
+            both = both + from_y[n].astype(F32)
+        both = both * scale
+        gate, up = both[:, :width], both[:, width:]
+        hid[c, y] = (gate / (1.0 + jnp.exp(-gate)) * up).astype(BF16)
+        for oy in FAR_Y:
+            send(hid.at[c, y], hid.at[c, y], hy_ss, hy_rs.at[oy - 1], at(dy=oy))
+        send(hid.at[c, y], hid.at[c, y], hc_ss, hc_rs, at(flip=True))
+        later(hid.at[0, pl.ds(0, 3)], hy_ss)
+        later(hid.at[0], hc_ss)
+    for hid, _, hy_rs, hc_ss, hc_rs in hids:
+        for oy in (1, 3, 2):
+            yy = (y + NY - oy) % NY
+            wait_bytes(hid.at[c, yy], hy_rs.at[oy - 1])
+            send(hid.at[c, yy], hid.at[c, yy], hc_ss, hc_rs, at(flip=True))
+    for hid, _, _, _, hc_rs in hids:
+        wait_bytes(hid.at[1 - c], hc_rs)
+
+    loads[4].wait()
 
     def out_a(part, lowered):
         first, width = PARTS_A[part]
@@ -524,7 +526,10 @@
         out_ref[:, FIRST_B:] = (gat_b[x, z].astype(F32) + lowered).astype(BF16)
 
     sum_over_dp(
-        lambda xx: hid[xx // 2, pl.ds((xx % 2) * 2, 2)].reshape(128, FFD), lambda: hid[...].reshape(512, FFD), wd_v,
+        lambda xx: jnp.concatenate(
+            [hid[0][xx // 2, pl.ds((xx % 2) * 2, 2)].reshape(128, -1) for hid in hids], axis=1
+        ),
+        lambda: jnp.concatenate([hid[0][...].reshape(512, -1) for hid in hids], axis=1), wd_v,
         lambda zz: zz, sums[1], out_a, False, out_b,
     )
     for end in ends:
@@ -553,7 +558,7 @@
 
     scratch = [
         V((256, COLS), BF16), V((TOK, COLS, 128), BF16), V((128, TOK, COLS), BF16), V((HEADS, KL, VH), BF16),
-        V((512, WIDTH), BF16), V((2 * FFD, WIDTH), BF16), V((WIDTH, 2 * FFD), BF16), V((FFD, WIDTH), BF16), dma((7,)),
+        V((512, WIDTH), BF16), V((2 * FFD, WIDTH), BF16), V((WIDTH, 2 * FFD), BF16), V((FFD, WIDTH), BF16), dma((9,)),
         V((1, 1, 128), I32), V((32, 1, 128), I32), pltpu.SMEM((32, 1, 128), I32),
         V((1, 1, 256), I32), pltpu.SMEM((1, 1, 256), I32), V((REQ_D, 256), F32), dma((2,)), one, one,
         [V((32, 16, w), BF16) for _, w in PARTS], [V((32, 16, w), BF16) for _, w in PARTS], dma((n,)), dma((n,)),
@@ -565,9 +570,12 @@
         [[V((NX, NZ, REQ_D, w), BF16), one, one, one, dma((3,))] for _, w in PARTS_A],
         V((NX, NZ, REQ_D, WB), BF16), one, one, V((NX, REQ_D, WB), BF16), one, one,
         V((8, 64, WIDTH), BF16), V((NX, 1, 128), F32), V((7, NX, 1, 128), F32), one, one,
-        V((2, 2, 64, 2 * FFD), F32), V((2, 2, 64, 2 * FFD), BF16), V((2, 2, 64, 2 * FFD), BF16), one, dma((2,)),
-        V((3, 64, 2 * FFD), BF16), V((3, 64, 2 * FFD), BF16), one, one,
-        V((NC, NY, 64, FFD), BF16), one, dma((3,)), one, one,
+        [
+            [V((NY, 64, 2 * w), F32), V((NY, 64, 2 * w), BF16), V((NY, 64, 2 * w), BF16), one, one,
+             V((3, 64, 2 * w), BF16), V((3, 64, 2 * w), BF16), one, one]
+            for _, w in UNITS
+        ],
+        [[V((NC, NY, 64, w), BF16), one, dma((3,)), one, one] for _, w in UNITS],
     ]
     return pl.pallas_call(
         kernel,

time: 123 us -> 121 us (0.984)
  Pallas kernels: 122 us -> 120 us
    pallas_call x1, Pallas kernels: 122 us -> 120 us  [per_device(): pl.pallas_call(kernel, out_shape=jax.ShapeDtypeStruct((REQ_D, WIDTH), BF1...]
where the time goes in v5:
time: 121 us
  Pallas kernels  120 us (99%)
  local copies, waits for them, and re-layouts  1.36 us (1%)
    pallas_call x1, Pallas kernels, per_device(): pl.pallas_call(kernel, out_shape=jax.ShapeDtypeStruct((REQ_D, WIDTH), BF1...  120 us

profile of v5, /device:TPU:1, one launch (start us, length us, event | category | flops | bytes accessed | tf_op | source)
XLA Modules:
  0.0 121.2 jit_solution(2702836606909716108)
XLA Ops:
  0.0 119.8 %layer.1 = bf16[16,896]{1,0:T(8,128)(2,1)} custom-call(s32[4,16]{1,0:T(4,128)} %bitcast.12, s32[4,16]{1,0:T(4,128)} %bitcast.13, s32[1,16]{1,0:T(1,128)} %bitcast.14, s32[1,16]{1,0:T(1,128)} %bitcast.15, bf16[16,576]{1,0:T(8,128)(2,1)} %nl_ref.1, bf16[16,896]{1,0:T(8,128)(2,1)} %resid_ref.1, f32[896]{0:T(1024)} %gain_ref.1, bf16[256,576]{1,0:T(8,128)(2,1)} %bitcast.11, ...), custom_call_target="tpu_custom_call" | custom-call | tf_op jit(solution)/shard_map/layer/pallas_call | solution.py:580
  119.8 1.4 %copy.16 = bf16[16,896]{1,0:T(8,128)(2,1)} copy(bf16[16,896]{1,0:T(8,128)(2,1)} %layer.1) | data formatting | bytes 57344

commit v6 on v5

--- a/solution.py
+++ b/solution.py
@@ -23,7 +23,7 @@
 WIDTH = 896
 PARTS_A, FIRST_B = ((0, 384), (384, 256)), 640
 WB = WIDTH - FIRST_B
-UNITS = ((0, 256), (256, 320))
+UNITS = ((0, 256), (256, 256), (512, 64))
 PARTS = ((0, 256), (256, 256), (512, 64))
 FFD = 576
 D = 7168
@@ -438,31 +438,37 @@
         later(gat.at[pl.ds(0, 3)], x_ss)
 
     def widen(block, gain):
-        block = block.astype(F32)
-        square = block * block
-        high = square.astype(BF16)
-        low = (square - high.astype(F32)).astype(BF16)
-        ones = jnp.ones((8, block.shape[1]), BF16)
-        return (block * gain).astype(BF16), (dot_t(ones, high) + dot_t(ones, low))[0:1]
+        return (block.astype(F32) * gain).astype(BF16)
+
+    def square_sums():
+        for xx in range(NX):
+            total = jnp.zeros((8, 128), F32)
+            for gat in [gat[0] for gat in gat_a] + [gat_b]:
+                block = gat[xx].reshape(128, -1).astype(F32)
+                square = block * block
+                high = square.astype(BF16)
+                low = (square - high.astype(F32)).astype(BF16)
+                ones = jnp.ones((8, block.shape[1]), BF16)
+                total = total + dot_t(ones, high) + dot_t(ones, low)
+            ssq_send[xx] = total[0:1]
+        tp_others = [(2, True), (2, False), (1, True), (3, True), (1, False), (3, False), (0, True)]
+        for n, (oy, flip) in enumerate(tp_others):
+            send(ssq_send, ssq_recv.at[n], ssq_ss, ssq_rs, at(dy=oy, flip=flip))
+        later(ssq_recv, ssq_ss)
 
     gain = gain_ref[...].reshape(1, WIDTH)
 
-    for part, ((first, width), (gat, _, _, _, x_rs)) in enumerate(zip(PARTS_A, gat_a)):
+    for (first, width), (gat, _, _, _, x_rs) in zip(PARTS_A, gat_a):
         for ox in (0, 1, 3, 2):
             xx = (x + NX - ox) % NX
             if ox:
                 wait_bytes(gat.at[xx], x_rs.at[ox - 1])
-            act, squares = widen(gat[xx].reshape(128, width), gain[:, first : first + width])
+            act = widen(gat[xx].reshape(128, width), gain[:, first : first + width])
             act_v[pl.ds(xx * 2, 2), :, first : first + width] = act.reshape(2, 64, width)
-            ssq_send[xx] = ssq_send[xx] + squares if part else squares
     wait_bytes(gat_b.at[:, pl.ds(0, 7)], gbz_rs)
     for xx in range(NX):
-        act, squares = widen(gat_b[xx].reshape(128, WB), gain[:, FIRST_B:])
+        act = widen(gat_b[xx].reshape(128, WB), gain[:, FIRST_B:])
         act_v[2 * xx : 2 * xx + 2, :, FIRST_B:] = act.reshape(2, 64, WB)
-        ssq_send[xx] = ssq_send[xx] + squares
-    for n, (oy, flip) in enumerate([(2, True), (2, False), (1, True), (3, True), (1, False), (3, False), (0, True)]):
-        send(ssq_send, ssq_recv.at[n], ssq_ss, ssq_rs, at(dy=oy, flip=flip))
-    later(ssq_recv, ssq_ss)
 
     ways = (2, 1, 3, 0)
 
@@ -476,6 +482,8 @@
         send(to_core, from_core, core_ss, core_rs, at(flip=True))
         later(to_core, core_ss)
         own[...] = products(c, part)
+        if part == 1:
+            square_sums()
         wait_bytes(from_core, core_rs)
         for n in range(3):
             to_y[n] = (own[n] + from_core[n].astype(F32)).astype(BF16)
@@ -558,7 +566,7 @@
 
     scratch = [
         V((256, COLS), BF16), V((TOK, COLS, 128), BF16), V((128, TOK, COLS), BF16), V((HEADS, KL, VH), BF16),
-        V((512, WIDTH), BF16), V((2 * FFD, WIDTH), BF16), V((WIDTH, 2 * FFD), BF16), V((FFD, WIDTH), BF16), dma((9,)),
+        V((512, WIDTH), BF16), V((2 * FFD, WIDTH), BF16), V((WIDTH, 2 * FFD), BF16), V((FFD, WIDTH), BF16), dma((5 + 2 * len(UNITS),)),
         V((1, 1, 128), I32), V((32, 1, 128), I32), pltpu.SMEM((32, 1, 128), I32),
         V((1, 1, 256), I32), pltpu.SMEM((1, 1, 256), I32), V((REQ_D, 256), F32), dma((2,)), one, one,
         [V((32, 16, w), BF16) for _, w in PARTS], [V((32, 16, w), BF16) for _, w in PARTS], dma((n,)), dma((n,)),

time: 121 us -> 121 us (level)
  no operation moved by 1% of the time
where the time goes in v6:
time: 121 us
  Pallas kernels  119 us (98%)
  local copies, waits for them, and re-layouts  1.36 us (1%)
    pallas_call x1, Pallas kernels, per_device(): pl.pallas_call(kernel, out_shape=jax.ShapeDtypeStruct((REQ_D, WIDTH), BF1...  119 us

profile of v6, /device:TPU:1, one launch (start us, length us, event | category | flops | bytes accessed | tf_op | source)
XLA Modules:
  0.0 120.6 jit_solution(6173957726245794987)
XLA Ops:
  0.0 119.2 %layer.1 = bf16[16,896]{1,0:T(8,128)(2,1)} custom-call(s32[4,16]{1,0:T(4,128)} %bitcast.12, s32[4,16]{1,0:T(4,128)} %bitcast.13, s32[1,16]{1,0:T(1,128)} %bitcast.14, s32[1,16]{1,0:T(1,128)} %bitcast.15, bf16[16,576]{1,0:T(8,128)(2,1)} %nl_ref.1, bf16[16,896]{1,0:T(8,128)(2,1)} %resid_ref.1, f32[896]{0:T(1024)} %gain_ref.1, bf16[256,576]{1,0:T(8,128)(2,1)} %bitcast.11, ...), custom_call_target="tpu_custom_call" | custom-call | tf_op jit(solution)/shard_map/layer/pallas_call | solution.py:588
  119.2 1.4 %copy.16 = bf16[16,896]{1,0:T(8,128)(2,1)} copy(bf16[16,896]{1,0:T(8,128)(2,1)} %layer.1) | data formatting | bytes 57344

commit v7 on v6

--- a/solution.py
+++ b/solution.py
@@ -477,11 +477,17 @@
         act = jnp.concatenate([act_v[half * 4 + (y + oy) % NY] for oy in ways], axis=0)
         return dot(act, wt_v[:, 2 * first : 2 * (first + width)]).reshape(NY, 64, 2 * width)
 
-    for part, (own, to_core, from_core, core_ss, core_rs, to_y, from_y, y_ss, y_rs) in enumerate(units):
+    def start_part(part):
+        _, to_core, from_core, core_ss, core_rs, *_ = units[part]
         to_core[...] = products(1 - c, part).astype(BF16)
         send(to_core, from_core, core_ss, core_rs, at(flip=True))
         later(to_core, core_ss)
+
+    start_part(0)
+    for part, (own, _, from_core, _, core_rs, to_y, from_y, y_ss, y_rs) in enumerate(units):
         own[...] = products(c, part)
+        if part + 1 < len(units):
+            start_part(part + 1)
         if part == 1:
             square_sums()
         wait_bytes(from_core, core_rs)

time: 121 us -> 121 us (level)
  no operation moved by 1% of the time
where the time goes in v7:
time: 121 us
  Pallas kernels  119 us (98%)
  local copies, waits for them, and re-layouts  1.36 us (1%)
    pallas_call x1, Pallas kernels, per_device(): pl.pallas_call(kernel, out_shape=jax.ShapeDtypeStruct((REQ_D, WIDTH), BF1...  119 us

profile of v7, /device:TPU:1, one launch (start us, length us, event | category | flops | bytes accessed | tf_op | source)
XLA Modules:
  0.0 120.8 jit_solution(17063235607695523862)
XLA Ops:
  0.0 119.4 %layer.1 = bf16[16,896]{1,0:T(8,128)(2,1)} custom-call(s32[4,16]{1,0:T(4,128)} %bitcast.12, s32[4,16]{1,0:T(4,128)} %bitcast.13, s32[1,16]{1,0:T(1,128)} %bitcast.14, s32[1,16]{1,0:T(1,128)} %bitcast.15, bf16[16,576]{1,0:T(8,128)(2,1)} %nl_ref.1, bf16[16,896]{1,0:T(8,128)(2,1)} %resid_ref.1, f32[896]{0:T(1024)} %gain_ref.1, bf16[256,576]{1,0:T(8,128)(2,1)} %bitcast.11, ...), custom_call_target="tpu_custom_call" | custom-call | tf_op jit(solution)/shard_map/layer/pallas_call | solution.py:594
  119.4 1.4 %copy.16 = bf16[16,896]{1,0:T(8,128)(2,1)} copy(bf16[16,896]{1,0:T(8,128)(2,1)} %layer.1) | data formatting | bytes 57344
